TPU v7x, 128 devices: a whole 4x4x4 slice. The times are simulated.
128 devices in a mesh: space: 8 (over y, core), energy: 16 (over z, x).
Axes of the slice: x: 4, y: 4, z: 4, core: 2. Of those that a mesh axis runs over, the one named last changes fastest.
Arguments:
- ham_diag: float32 [16, 2, 128, 128], P('space'), may hold values from -0.5 to 0.5
- coupling: float32 [16, 2, 128, 128], P('space'), may hold values from -0.5 to 0.5
- contact_left: float32 [2, 128, 128], replicated, may hold values from -0.5 to 0.5
- mode_weight: float32 [4], replicated, may hold values from 0.5 to 2
- mode_offset: int32 [4], replicated, may hold values from -8 to 8, as said below
- pattern: int32 [128, 128], replicated, may hold values 0 or 1
Outputs:
- sigma: float32 [16, 16, 2, 128, 128], P('energy', 'space')
Inputs may be any that keep to these rules, and one draw needn't show every extreme that they name: `mode_offset`: the offsets are -1, 1, -8 and 8 in some order.
All inputs are finite; a program needn't handle non-finite values.
Results may differ from a plain program's by a relative error of at most 0.0003.
Values sent between devices are 32-bit elements; how exact they have to be, the bound alone decides.
A program may use at most 64 MiB of HBM per device.

v0:
```python
import jax
import jax.numpy as jnp
from jax import lax
from jax.sharding import PartitionSpec as P

E_DEV = 1


HIGHEST = lax.Precision.HIGHEST
BROADENING = 0.1


def carried_in(value, axis, join, neutral, backward):
    count, mine = (lax.axis_size(axis), lax.axis_index(axis))
    pieces = jax.tree.map(lambda part: lax.all_gather(part, axis), value)
    if backward:
        pieces = jax.tree.map(lambda part: part[::-1], pieces)
        mine = count - 1 - mine
    subtotal = jax.tree.map(
        lambda part, zero: jnp.full_like(part, 0) + jnp.asarray(zero, part.dtype), value, neutral
    )

    def lap(position, subtotal):
        longer = join(subtotal, jax.tree.map(lambda part: part[position], pieces))
        return jax.tree.map(lambda new, old: jnp.where(position < mine, new, old), longer, subtotal)

    return lax.fori_loop(0, count - 1, lap, subtotal)


def real_form_of(matrix):
    return jnp.concatenate(
        [jnp.concatenate([matrix[0], -matrix[1]], 1), jnp.concatenate([matrix[1], matrix[0]], 1)], 0
    )


def product(former, latter):
    order_size = former.shape[1]
    stacked = jnp.concatenate([latter[0], latter[1]], 0)
    joined = jnp.dot(real_form_of(former), stacked, precision=HIGHEST)
    return joined.reshape(2, order_size, latter.shape[2])


def adjoint(matrix):
    return jnp.stack([matrix[0].T, -matrix[1].T])


def times_imag(matrix):
    return jnp.stack([-matrix[1], matrix[0]])


def hermitian(matrix):
    return 0.5 * (matrix + adjoint(matrix))


def unit_block(order_size):
    identity_real = jnp.eye(order_size, dtype=jnp.float32)
    return jnp.stack([identity_real, jnp.zeros_like(identity_real)])


def invert(matrix):
    order_size = matrix.shape[1]
    real_form = real_form_of(matrix)
    normal = jnp.dot(real_form.T, real_form, precision=HIGHEST)
    factor = jnp.linalg.cholesky(normal)
    rough = jax.scipy.linalg.cho_solve((factor, True), real_form.T[:, :order_size])
    start_guess = jnp.stack([rough[:order_size], rough[order_size:]])
    residue = unit_block(order_size) - product(matrix, start_guess)
    return start_guess + product(start_guess, residue)


def green_diagonal(blocks, links):

    def forward_step(previous, element):
        diag_block, bridge = element
        fresh = invert(diag_block - product(adjoint(bridge), product(previous, bridge)))
        return (fresh, fresh)

    first = invert(blocks[0])
    later = lax.scan(forward_step, first, (blocks[1:], links))[1]
    left_green = jnp.concatenate([first[None], later], 0)

    def backward_step(following, element):
        left_block, bridge = element
        reach = product(left_block, bridge)
        back_reach = product(adjoint(bridge), left_block)
        full = left_block + product(reach, product(following, back_reach))
        return (full, full)

    inner = lax.scan(backward_step, left_green[-1], (left_green[:-1], links), reverse=True)[1]
    return jnp.concatenate([inner, left_green[-1:]], 0)


def segment_corners(blocks, links):
    start_green = invert(blocks[0])

    def extend(corner_state, element):
        head_head, head_tail, tail_head, tail_tail = corner_state
        diag_block, bridge = element
        bridge_adj = adjoint(bridge)
        fresh = invert(diag_block - product(bridge_adj, product(tail_tail, bridge)))
        new_head_tail = product(product(head_tail, bridge), fresh)
        back_link = product(bridge_adj, tail_head)
        new_head_head = head_head + product(new_head_tail, back_link)
        new_tail_head = product(fresh, back_link)
        return ((new_head_head, new_head_tail, new_tail_head, fresh), None)

    return lax.scan(
        extend, (start_green, start_green, start_green, start_green), (blocks[1:], links)
    )[0]


def join_pair(former, latter, bridge):
    bridge_adj = adjoint(bridge)
    left_part = product(former[3], bridge)
    right_part = product(latter[0], bridge_adj)
    resolvent = invert(unit_block(bridge.shape[1]) - product(left_part, right_part))
    across = product(resolvent, former[2])
    former_reach = product(former[1], bridge)
    latter_reach = product(latter[2], bridge_adj)
    head_head = former[0] + product(former_reach, product(right_part, across))
    tail_head = product(latter_reach, across)
    inner_part = latter[1] + product(right_part, product(resolvent, product(left_part, latter[1])))
    head_tail = product(former_reach, inner_part)
    tail_tail = latter[3] + product(latter_reach, product(left_part, inner_part))
    return (head_head, head_tail, tail_head, tail_tail)


def join(former, latter):
    merged = jax.vmap(join_pair, in_axes=(0, 0, None))(former[:4], latter[:4], former[4])
    former_full = former[5] > 0
    latter_full = latter[5] > 0
    chosen = tuple(
        (
            jnp.where(former_full, jnp.where(latter_full, joined, former_item), latter_item)
            for joined, former_item, latter_item in zip(merged, former[:4], latter[:4])
        )
    )
    bridge = jnp.where(latter_full, latter[4], former[4])
    return chosen + (bridge, jnp.maximum(former[5], latter[5]))


def join_reversed(higher, lower):
    return join(lower, higher)


def mode_table(targets, sources, mode_weight, mode_offset):
    hits = (sources[None, :, None] == targets[:, None, None] - mode_offset[None, None, :]).astype(
        jnp.float32
    )
    return jnp.sum(hits * mode_weight[None, None, :], axis=2)


def on_device(ham_diag, coupling, contact_left, mode_weight, mode_offset, pattern):
    order_size = ham_diag.shape[-1]
    space_count = lax.axis_size("space")
    position = lax.axis_index("space")
    energy_count = lax.axis_size("energy")
    energy_rank = lax.axis_index("energy")
    energy_total = E_DEV * energy_count
    local_grid = energy_rank * E_DEV + jnp.arange(E_DEV, dtype=jnp.int32)
    energies = -2.0 + 4.0 * (local_grid.astype(jnp.float32) + 0.5) / energy_total
    unit = unit_block(order_size)
    shifts = energies[:, None, None, None] * unit[None] + BROADENING * times_imag(unit)[None]
    onsite = -jax.vmap(hermitian)(ham_diag)
    first_mask = (position == 0).astype(jnp.float32)
    last_mask = (position == space_count - 1).astype(jnp.float32)
    left_contact = times_imag(0.5 * product(contact_left, adjoint(contact_left)))
    right_contact = times_imag(0.5 * product(adjoint(coupling[-1]), coupling[-1]))
    onsite = onsite.at[0].add(first_mask * left_contact).at[-1].add(last_mask * right_contact)
    blocks = onsite[None] + shifts[:, None]
    links = coupling[:-1]
    outgoing = coupling[-1]
    corners = jax.vmap(segment_corners, in_axes=(0, None))(blocks, links)
    filled = jnp.ones((), jnp.float32)
    segment = tuple(corners) + (outgoing, filled)
    empty = tuple((jnp.zeros_like(member) for member in segment))
    before = carried_in(segment, "space", join, empty, False)
    after = carried_in(segment, "space", join_reversed, empty, True)
    in_link = before[4]
    sigma_before = jax.vmap(lambda corner: product(adjoint(in_link), product(corner, in_link)))(
        before[3]
    )
    sigma_after = jax.vmap(lambda corner: product(outgoing, product(corner, adjoint(outgoing))))(
        after[0]
    )
    bounded = blocks.at[:, 0].add(-sigma_before).at[:, -1].add(-sigma_after)
    green = jax.vmap(green_diagonal, in_axes=(0, None))(bounded, links)
    targets = jnp.arange(lax.axis_size("energy") * E_DEV, dtype=jnp.int32)
    table = mode_table(targets, local_grid, mode_weight, mode_offset)
    summed = lax.psum_scatter(
        jnp.einsum("ef,fkxab->ekxab", table, green, precision=HIGHEST),
        "energy",
        scatter_dimension=0,
        tiled=True,
    )
    return summed * pattern.astype(jnp.float32)


def solution(mesh):
    placed = (P("space", None, None, None), P("space", None, None, None), P(), P(), P(), P())
    return jax.shard_map(
        on_device,
        mesh=mesh,
        in_specs=placed,
        out_specs=P("energy", "space", None, None, None),
        check_vma=False,
    )
```

profile of v0, /device:TPU:0, one launch (start us, length us, event | category | flops | bytes accessed | tf_op | source)
XLA Modules:
  0.0 1538.8 jit_solution(16849040394704365928)
XLA Ops:
  14.0 11.7 custom-call.46
  25.7 9.8 custom-call.47
  36.0 11.7 custom-call.48
  54.0 19.7 %custom-call.49 = f32[1,2,128,128]{2,3,1,0:T(8,128)S(1)} custom-call(f32[1,2,128,128]{3,2,1,0:T(8,128)S(1)} %bitcast.1749), custom_call_target="InvertDiagBlocksLowerTriangular" | custom-call | tf_op jit(solution)/shard_map/vmap(jit(_cho_solve))/triangular_solve | solution.py:65
  78.0 11.7 custom-call.50
  89.7 9.8 custom-call.51
  100.0 12.2 custom-call.52
  118.8 19.7 %custom-call.53 = f32[1,2,128,128]{2,3,1,0:T(8,128)S(1)} custom-call(f32[1,2,128,128]{3,2,1,0:T(8,128)S(1)} %bitcast.1750), custom_call_target="InvertDiagBlocksLowerTriangular" | custom-call | tf_op jit(solution)/shard_map/vmap()/while/body/eval_jaxpr/jit(_cho_solve)/triangular_solve | solution.py:65
  147.7 14.9 all-reduce.5
  168.5 25.1 %all-gather.17.cloned.1.call-done = f32[16,128,128]{2,1,0:T(8,128)} async-done(((f32[2,128,128]{2,1,0:T(8,128)}), f32[16,128,128]{2,1,0:T(8,128)}) %all-gather.17.cloned.1.call-update) | async-done | bytes 1048592 | tf_op jit(solution)/shard_map/all_gather | solution.py:15
  193.7 25.0 %all-gather.9.cloned.1.call-done = f32[8,1,2,128,128]{4,3,2,1,0:T(8,128)} async-done(((f32[1,1,2,128,128]{4,3,2,1,0:T(8,128)}), f32[8,1,2,128,128]{4,3,2,1,0:T(8,128)}) %all-gather.9.cloned.1.call-update) | async-done | bytes 1048592 | tf_op jit(solution)/shard_map/all_gather | solution.py:15
  218.7 24.8 %all-gather.13.cloned.1.call-done = f32[16,128,128]{2,1,0:T(8,128)} async-done(((f32[2,128,128]{2,1,0:T(8,128)}), f32[16,128,128]{2,1,0:T(8,128)}) %all-gather.13.cloned.1.call-update) | async-done | bytes 1048592 | tf_op jit(solution)/shard_map/all_gather | solution.py:15
  243.5 24.8 %all-gather.11.cloned.1.call-done = f32[8,2,128,128]{3,2,1,0:T(8,128)} async-done(((f32[1,2,128,128]{3,2,1,0:T(8,128)}), f32[8,2,128,128]{3,2,1,0:T(8,128)}) %all-gather.11.cloned.1.call-update) | async-done | bytes 1048592 | tf_op jit(solution)/shard_map/all_gather | solution.py:15
  268.3 523.7 %while.70 = (s32[]{:T(128)}, f32[1,2,128,128]{3,2,1,0:T(8,128)S(1)}, f32[2,128,128]{2,1,0:T(8,128)S(1)}, f32[]{:T(128)}, s32[]{:T(128)}, /*index=5*/f32[8]{0:T(1...) while((s32[]{:T(128)}, ...), condition=%wide.region_6.9_spmd.clone, body=%wide.region_5.8_spmd.clone.sunk | while | flops 1513521408 | bytes 24627640 | solution.py:27
  273.9 11.7 custom-call.74
  295.9 11.7 custom-call.76
  314.7 19.7 %custom-call.78 = f32[1,2,128,128]{2,3,1,0:T(8,128)S(1)} custom-call(f32[1,2,128,128]{3,2,1,0:T(8,128)S(1)} %bitcast.1752), custom_call_target="InvertDiagBlocksLowerTriangular" | custom-call | tf_op jit(solution)/shard_map/while/body/eval_jaxpr/vmap(jit(_cho_solve))/triangular_solve | solution.py:65
  348.6 11.7 custom-call.74
  370.7 11.7 custom-call.76
  389.5 19.7 %custom-call.78 = f32[1,2,128,128]{2,3,1,0:T(8,128)S(1)} custom-call(f32[1,2,128,128]{3,2,1,0:T(8,128)S(1)} %bitcast.1752), custom_call_target="InvertDiagBlocksLowerTriangular" | custom-call | tf_op jit(solution)/shard_map/while/body/eval_jaxpr/vmap(jit(_cho_solve))/triangular_solve | solution.py:65
  423.4 11.7 custom-call.74
  445.4 11.7 custom-call.76
  464.2 19.7 %custom-call.78 = f32[1,2,128,128]{2,3,1,0:T(8,128)S(1)} custom-call(f32[1,2,128,128]{3,2,1,0:T(8,128)S(1)} %bitcast.1752), custom_call_target="InvertDiagBlocksLowerTriangular" | custom-call | tf_op jit(solution)/shard_map/while/body/eval_jaxpr/vmap(jit(_cho_solve))/triangular_solve | solution.py:65
  498.1 11.7 custom-call.74
  520.2 11.7 custom-call.76
  539.0 19.7 %custom-call.78 = f32[1,2,128,128]{2,3,1,0:T(8,128)S(1)} custom-call(f32[1,2,128,128]{3,2,1,0:T(8,128)S(1)} %bitcast.1752), custom_call_target="InvertDiagBlocksLowerTriangular" | custom-call | tf_op jit(solution)/shard_map/while/body/eval_jaxpr/vmap(jit(_cho_solve))/triangular_solve | solution.py:65
  572.8 11.7 custom-call.74
  594.9 11.7 custom-call.76
  613.7 19.7 %custom-call.78 = f32[1,2,128,128]{2,3,1,0:T(8,128)S(1)} custom-call(f32[1,2,128,128]{3,2,1,0:T(8,128)S(1)} %bitcast.1752), custom_call_target="InvertDiagBlocksLowerTriangular" | custom-call | tf_op jit(solution)/shard_map/while/body/eval_jaxpr/vmap(jit(_cho_solve))/triangular_solve | solution.py:65
  647.6 11.7 custom-call.74
  669.6 11.7 custom-call.76
  688.4 19.7 %custom-call.78 = f32[1,2,128,128]{2,3,1,0:T(8,128)S(1)} custom-call(f32[1,2,128,128]{3,2,1,0:T(8,128)S(1)} %bitcast.1752), custom_call_target="InvertDiagBlocksLowerTriangular" | custom-call | tf_op jit(solution)/shard_map/while/body/eval_jaxpr/vmap(jit(_cho_solve))/triangular_solve | solution.py:65
  722.3 11.7 custom-call.74
  744.4 11.7 custom-call.76
  763.2 19.7 %custom-call.78 = f32[1,2,128,128]{2,3,1,0:T(8,128)S(1)} custom-call(f32[1,2,128,128]{3,2,1,0:T(8,128)S(1)} %bitcast.1752), custom_call_target="InvertDiagBlocksLowerTriangular" | custom-call | tf_op jit(solution)/shard_map/while/body/eval_jaxpr/vmap(jit(_cho_solve))/triangular_solve | solution.py:65
  793.8 11.7 custom-call.54
  816.5 12.5 custom-call.56
  835.9 19.7 %custom-call.57 = f32[1,2,128,128]{2,3,1,0:T(8,128)S(1)} custom-call(f32[1,2,128,128]{3,2,1,0:T(8,128)S(1)} %bitcast.1751), custom_call_target="InvertDiagBlocksLowerTriangular" | custom-call | tf_op jit(solution)/shard_map/vmap(jit(_cho_solve))/triangular_solve | solution.py:65
  869.9 509.2 %while.72 = (s32[]{:T(128)}, f32[1,2,128,128]{3,2,1,0:T(8,128)S(1)}, f32[]{:T(128)}, s32[]{:T(128)}, f32[8]{0:T(128)}, /*index=5*/f32[8,1,2,128,128]{4,3,2,1,0:T...) while((s32[]{:T(128)}, ...), condition=%wide.region_8.11_spmd.clone, body=%wide.region_7.10_spmd.clone.sunk | while | flops 1311998208 | bytes 22596184 | solution.py:27
  874.4 11.7 custom-call.79
  896.5 11.7 custom-call.81
  914.7 19.7 %custom-call.83 = f32[1,2,128,128]{2,3,1,0:T(8,128)S(1)} custom-call(f32[1,2,128,128]{3,2,1,0:T(8,128)S(1)} %bitcast.1753), custom_call_target="InvertDiagBlocksLowerTriangular" | custom-call | tf_op jit(solution)/shard_map/while/body/eval_jaxpr/vmap(jit(_cho_solve))/triangular_solve | solution.py:65
  947.1 11.7 custom-call.79
  969.2 11.7 custom-call.81
  987.4 19.7 %custom-call.83 = f32[1,2,128,128]{2,3,1,0:T(8,128)S(1)} custom-call(f32[1,2,128,128]{3,2,1,0:T(8,128)S(1)} %bitcast.1753), custom_call_target="InvertDiagBlocksLowerTriangular" | custom-call | tf_op jit(solution)/shard_map/while/body/eval_jaxpr/vmap(jit(_cho_solve))/triangular_solve | solution.py:65
  1019.8 11.7 custom-call.79
  1041.9 11.7 custom-call.81
  1060.1 19.7 %custom-call.83 = f32[1,2,128,128]{2,3,1,0:T(8,128)S(1)} custom-call(f32[1,2,128,128]{3,2,1,0:T(8,128)S(1)} %bitcast.1753), custom_call_target="InvertDiagBlocksLowerTriangular" | custom-call | tf_op jit(solution)/shard_map/while/body/eval_jaxpr/vmap(jit(_cho_solve))/triangular_solve | solution.py:65
  1092.5 11.7 custom-call.79
  1114.6 11.7 custom-call.81
  1132.8 19.7 %custom-call.83 = f32[1,2,128,128]{2,3,1,0:T(8,128)S(1)} custom-call(f32[1,2,128,128]{3,2,1,0:T(8,128)S(1)} %bitcast.1753), custom_call_target="InvertDiagBlocksLowerTriangular" | custom-call | tf_op jit(solution)/shard_map/while/body/eval_jaxpr/vmap(jit(_cho_solve))/triangular_solve | solution.py:65
  1165.2 11.7 custom-call.79
  1187.2 11.7 custom-call.81
  1205.5 19.7 %custom-call.83 = f32[1,2,128,128]{2,3,1,0:T(8,128)S(1)} custom-call(f32[1,2,128,128]{3,2,1,0:T(8,128)S(1)} %bitcast.1753), custom_call_target="InvertDiagBlocksLowerTriangular" | custom-call | tf_op jit(solution)/shard_map/while/body/eval_jaxpr/vmap(jit(_cho_solve))/triangular_solve | solution.py:65
  1237.9 11.7 custom-call.79
  1259.9 11.7 custom-call.81
  1278.1 19.7 %custom-call.83 = f32[1,2,128,128]{2,3,1,0:T(8,128)S(1)} custom-call(f32[1,2,128,128]{3,2,1,0:T(8,128)S(1)} %bitcast.1753), custom_call_target="InvertDiagBlocksLowerTriangular" | custom-call | tf_op jit(solution)/shard_map/while/body/eval_jaxpr/vmap(jit(_cho_solve))/triangular_solve | solution.py:65
  1310.6 11.7 custom-call.79
  1332.6 11.7 custom-call.81
  1350.8 19.7 %custom-call.83 = f32[1,2,128,128]{2,3,1,0:T(8,128)S(1)} custom-call(f32[1,2,128,128]{3,2,1,0:T(8,128)S(1)} %bitcast.1753), custom_call_target="InvertDiagBlocksLowerTriangular" | custom-call | tf_op jit(solution)/shard_map/while/body/eval_jaxpr/vmap(jit(_cho_solve))/triangular_solve | solution.py:65
  1385.5 11.7 custom-call.58
  1407.6 11.9 custom-call.60
  1426.3 19.7 %custom-call.61 = f32[1,2,128,128]{2,3,1,0:T(8,128)S(1)} custom-call(f32[1,2,128,128]{3,2,1,0:T(8,128)S(1)} %bitcast.1748), custom_call_target="InvertDiagBlocksLowerTriangular" | custom-call | tf_op jit(solution)/shard_map/vmap()/while/body/eval_jaxpr/jit(_cho_solve)/triangular_solve | solution.py:65
  1452.1 77.8 %reduce-scatter.4.cloned.1.call-done = f32[1,2,2,128,128]{4,3,2,1,0:T(8,128)} async-done(((f32[16,2,2,128,128]{4,3,2,1,0:T(8,128)}), f32[1,2,2,128,128]{4,3,2,1,0:T(8,128)}) %reduce-scatter.4.cloned.1.call-update) | async-done | bytes 262160
  (1459 shorter events, 557.0 us)
Async XLA Ops:
  6.5 5.3 copy-start.17
  6.5 162.0 %all-gather.15.cloned.1.call-start = ((), (), s32[]{:S(2)}) async-start(), calls=%async_computation.4 | async-start | bytes 1179648 | tf_op jit(solution)/shard_map/all_gather | solution.py:15
  11.3 128.9 %copy-start.4 = (f32[1,128,128]{2,1,0:T(8,128)}, f32[1,128,128]{2,1,0:T(8,128)S(1)}, u32[]{:S(2)}) copy-start(f32[1,128,128]{2,1,0:T(8,128)S(1)} %fusion.238) | copy-start | bytes 196612
  12.0 0.6 copy-start.19
  12.1 151.2 %copy-start.18 = (f32[1,1,128,128]{2,3,1,0:T(8,128)}, f32[1,1,128,128]{2,3,1,0:T(8,128)S(1)}, u32[]{:S(2)}) copy-start(f32[1,1,128,128]{2,3,1,0:T(8,128)S(1)} %copy.239) | copy-start | bytes 196612
  13.2 779.5 %copy-start.6 = (f32[1,2,2,128,128]{3,4,2,1,0:T(8,128)}, f32[1,2,2,128,128]{3,4,2,1,0:T(8,128)S(1)}, u32[]{:S(2)}) copy-start(f32[1,2,2,128,128]{3,4,2,1,0:T(8,128)S(1)} %broadcast_add_fusion) | copy-start | bytes 786436
  76.2 62.5 %copy-start.9 = (f32[1,1,128,128]{2,3,1,0:T(8,128)}, f32[1,1,128,128]{2,3,1,0:T(8,128)S(1)}, u32[]{:S(2)}) copy-start(f32[1,1,128,128]{2,3,1,0:T(8,128)S(1)} %copy.242) | copy-start | bytes 196612
  76.3 1.0 copy-start.15
  139.5 6.9 copy-start.27
  140.1 24.1 %copy-start.22 = (f32[4]{0:T(128)S(1)}, f32[4]{0:T(128)}, u32[]{:S(2)}) copy-start(f32[4]{0:T(128)} %param.24) | copy-start | bytes 52
  140.2 24.0 %copy-start.23 = (s32[4]{0:T(128)S(1)}, s32[4]{0:T(128)}, u32[]{:S(2)}) copy-start(s32[4]{0:T(128)} %param.25) | copy-start | bytes 52
  141.0 4.1 copy-start.13
  142.5 51.2 %all-gather.17.cloned.1.call-start = ((), (), s32[]{:S(2)}) async-start(), calls=%async_computation.5 | async-start | bytes 1179648 | tf_op jit(solution)/shard_map/all_gather | solution.py:15
  143.2 1.2 copy-start.16
  144.3 74.4 %all-gather.9.cloned.1.call-start = ((), (), s32[]{:S(2)}) async-start(), calls=%async_computation.1 | async-start | bytes 1179648 | tf_op jit(solution)/shard_map/all_gather | solution.py:15
  145.0 98.5 %all-gather.13.cloned.1.call-start = ((), (), s32[]{:S(2)}) async-start(), calls=%async_computation.3 | async-start | bytes 1179648 | tf_op jit(solution)/shard_map/all_gather | solution.py:15
  145.6 122.7 %all-gather.11.cloned.1.call-start = ((), (), s32[]{:S(2)}) async-start(), calls=%async_computation.2 | async-start | bytes 1179648 | tf_op jit(solution)/shard_map/all_gather | solution.py:15
  146.3 1383.6 %reduce-scatter.4.cloned.1.call-start = ((), (), s32[]{:S(2)}) async-start(), calls=%async_computation.6 | async-start | bytes 4456448
  793.6 70.6 %copy-start.1 = (f32[8,1,2,128,128]{4,3,2,1,0:T(8,128)S(1)}, f32[8,1,2,128,128]{4,3,2,1,0:T(8,128)}, u32[]{:S(2)}) copy-start(f32[8,1,2,128,128]{4,3,2,1,0:T(8,128)} %get-tuple-element.1600) | copy-start | bytes 3145732
  815.6 49.6 %copy-start.2 = (f32[8,1,2,128,128]{4,3,2,1,0:T(8,128)S(1)}, f32[8,1,2,128,128]{4,3,2,1,0:T(8,128)}, u32[]{:S(2)}) copy-start(f32[8,1,2,128,128]{4,3,2,1,0:T(8,128)} %get-tuple-element.1602) | copy-start | bytes 3145732
  835.9 30.5 %copy-start.24 = (s32[2,2]{1,0:T(2,128)}, s32[2,2]{1,0:T(2,128)S(1)}, u32[]{:S(2)}) copy-start(s32[2,2]{1,0:T(2,128)S(1)} %get-tuple-element.1624) | copy-start | bytes 52
  857.2 2.0 copy-start.8
  859.2 8.6 copy-start
  862.9 0.7 copy-start.11
  866.3 2.5 copy-start.3
  869.9 511.5 %copy-start.10 = (f32[1,1,128,128]{2,3,1,0:T(8,128)S(1)}, f32[1,1,128,128]{2,3,1,0:T(8,128)}, u32[]{:S(2)}) copy-start(f32[1,1,128,128]{2,3,1,0:T(8,128)} %copy-done.9) | copy-start | bytes 196612
  869.9 514.1 %copy-start.7 = (f32[1,2,2,128,128]{3,4,2,1,0:T(8,128)S(1)}, f32[1,2,2,128,128]{3,4,2,1,0:T(8,128)}, u32[]{:S(2)}) copy-start(f32[1,2,2,128,128]{3,4,2,1,0:T(8,128)} %copy-done.6) | copy-start | bytes 786436
  869.9 514.1 %copy-start.14 = (f32[256,256]{1,0:T(8,128)S(1)}, f32[256,256]{1,0:T(8,128)}, u32[]{:S(2)}) copy-start(f32[256,256]{1,0:T(8,128)} %copy.222) | copy-start | bytes 786436
  936.5 3.1 copy-start.26
  1009.2 3.1 copy-start.26
  1081.9 3.1 copy-start.26
  1154.5 3.1 copy-start.26
  1227.2 3.1 copy-start.26
  1299.9 3.1 copy-start.26
  1372.6 3.1 copy-start.26
  1381.4 40.9 %copy-start.25 = (s32[2,2]{1,0:T(2,128)S(1)}, s32[2,2]{1,0:T(2,128)}, u32[]{:S(2)}) copy-start(s32[2,2]{1,0:T(2,128)} %copy-done.24) | copy-start | bytes 52
  1384.4 63.2 %copy-start.5 = (f32[1,128,128]{2,1,0:T(8,128)S(1)}, f32[1,128,128]{2,1,0:T(8,128)}, u32[]{:S(2)}) copy-start(f32[1,128,128]{2,1,0:T(8,128)} %copy-done.4) | copy-start | bytes 196612
  1422.3 26.8 %copy-start.12 = (f32[2,128,128]{2,1,0:T(8,128)S(1)}, f32[2,128,128]{2,1,0:T(8,128)}, u32[]{:S(2)}) copy-start(f32[2,128,128]{2,1,0:T(8,128)} %copy-done.11) | copy-start | bytes 393220
  1426.3 23.2 %copy-start.21 = (f32[16]{0:T(128)S(1)}, f32[16]{0:T(128)}, u32[]{:S(2)}) copy-start(f32[16]{0:T(128)} %select_reduce_fusion.8) | copy-start | bytes 196
  1449.5 2.6 copy-start.20
Sparse Core Ops, SparseCore 0:
  142.6 25.8 all-gather.14
  170.3 23.3 all-gather.16
  195.4 23.2 all-gather.8
  220.2 23.2 all-gather.12
  245.0 23.2 all-gather.10
  1452.2 77.6 reduce-scatter.3
where the time goes:
time: 1550 us; the launch traced here: 1540 us
  other arithmetic  1000 us (65%)
  waiting for transfers between devices  183 us (12%)
  local copies, waits for them, and re-layouts  143 us (9%)
  matrix products  133 us (9%)
  loops' own time  44.2 us (3%)
  between operations  20.7 us (1%)
    another operation x125, other arithmetic, invert(): factor = jnp.linalg.cholesky(normal)  624 us
    another operation x65, other arithmetic, invert(): jax.scipy.linalg.cho_solve((factor, True), real_form.T[:, :order_size])  355 us
    all_gather x5, waiting for transfers between devices, carried_in(): pieces = jax.tree.map(lambda part: lax.all_gather(part, axis), value)  104 us
    dot_general x165, matrix products, product(): joined = jnp.dot(real_form_of(former), stacked, precision=HIGHEST)  89.1 us
    unnamed x7, waiting for transfers between devices  79 us
    another operation x127, local copies, waits for them, and re-layouts, invert(): jax.scipy.linalg.cho_solve((factor, True), real_form.T[:, :order_size])  72.6 us
    another operation x2, loops' own time, carried_in(): return lax.fori_loop(0, count - 1, lap, subtotal)  43.3 us
  transfers between devices with their start and end apart: 6, of which 6 were waited for; matrix products, arithmetic and copies ran while one was open for 0% of the time, Pallas kernels for 0%

commit v1 on v0

v1 whole, which is shorter than its diff:
```python
import functools

import jax
import jax.numpy as jnp
from jax import lax
from jax.experimental import pallas as pl
from jax.experimental.pallas import tpu as pltpu
from jax.sharding import PartitionSpec as P

N = 128
PANEL = 16
ENERGIES = 16
BROADENING = 0.1
F32 = jnp.float32
MESH = pl.DeviceIdType.MESH
VM = pl.BlockSpec(memory_space=pltpu.VMEM)
HIGHEST = lax.Precision.HIGHEST
BLOCK = (2, N, N)


def split(x):
    high = x.astype(jnp.bfloat16)
    return high, (x - high.astype(F32)).astype(jnp.bfloat16)


def dot3(a, b):
    ah, al = split(a)
    bh, bl = split(b)
    d = functools.partial(jnp.dot, preferred_element_type=F32)
    return d(ah, bh) + (d(al, bh) + d(ah, bl))


def dot6(a, b):
    return jnp.dot(a, b, precision=HIGHEST, preferred_element_type=F32)


def mul(a, b, dot=dot6):
    left = jnp.concatenate([a[0], a[1]], 1)
    right = jnp.concatenate(
        [jnp.concatenate([b[0], b[1]], 1), jnp.concatenate([-b[1], b[0]], 1)], 0
    )
    out = dot(left, right)
    return out[:, :N], out[:, N:]


def add(a, b):
    return a[0] + b[0], a[1] + b[1]


def sub(a, b):
    return a[0] - b[0], a[1] - b[1]


def adj(a):
    return a[0].T, -a[1].T


def pick(cond, a, b):
    return jnp.where(cond, a[0], b[0]), jnp.where(cond, a[1], b[1])


def get(ref, *index):
    return ref[index + (0,)], ref[index + (1,)]


def put(ref, value, *index):
    ref[index + (0,)] = value[0]
    ref[index + (1,)] = value[1]


def rows8(x):
    return jnp.broadcast_to(x, (8, N))


def eliminate8(rr, ri, dr, di, g):
    row = lax.broadcasted_iota(jnp.int32, (8, N), 0)
    groups = len(rr)
    for k in range(8):
        pr, pi = rows8(dr[k][g][k : k + 1]), rows8(di[k][g][k : k + 1])
        inv = 1.0 / (pr * pr + pi * pi)
        qr, qi = pr * inv, -pi * inv
        at_pivot = row == k

        def step(xr, xi):
            ar, ai = rows8(xr[g][k : k + 1]), rows8(xi[g][k : k + 1])
            sr, si = qr * ar - qi * ai, qr * ai + qi * ar
            outr, outi = [], []
            for v in range(groups):
                yr = xr[v] - dr[k][v] * sr + di[k][v] * si
                yi = xi[v] - dr[k][v] * si - di[k][v] * sr
                if v == g:
                    yr, yi = jnp.where(at_pivot, sr, yr), jnp.where(at_pivot, si, yi)
                outr.append(yr)
                outi.append(yi)
            return outr, outi

        for j in range(k + 1, 8):
            dr[j], di[j] = step(dr[j], di[j])
        rr, ri = step(rr, ri)
    return rr, ri


def invert(ref):
    groups = PANEL // 8
    lane8 = lax.broadcasted_iota(jnp.int32, (8, N), 1)
    row8 = lax.broadcasted_iota(jnp.int32, (8, N), 0)
    lane = lax.broadcasted_iota(jnp.int32, (N, N), 1)
    for first in range(0, N, PANEL):
        span = [pl.ds(first + 8 * v, 8) for v in range(groups)]
        rr = [ref[0, s, :] for s in span]
        ri = [ref[1, s, :] for s in span]
        for g in range(groups):
            c0 = first + 8 * g
            dr = [[rows8_lane(rr[v], c0 + j) for v in range(groups)] for j in range(8)]
            di = [[rows8_lane(ri[v], c0 + j) for v in range(groups)] for j in range(8)]
            here = (lane8 >= c0) & (lane8 < c0 + 8)
            unit = jnp.where(lane8 - c0 == row8, 1.0, 0.0)
            rr = [jnp.where(here, unit if v == g else 0.0, rr[v]) for v in range(groups)]
            ri = [jnp.where(here, 0.0, ri[v]) for v in range(groups)]
            rr, ri = eliminate8(rr, ri, dr, di, g)
        pr, pi = jnp.concatenate(rr, 0), jnp.concatenate(ri, 0)

        def gap(rows):
            return [jnp.zeros((rows, 2 * N), F32)] if rows else []

        right = jnp.concatenate(
            gap(first)
            + [jnp.concatenate([pr, pi], 1)]
            + gap(N - PANEL)
            + [jnp.concatenate([-pi, pr], 1)]
            + gap(N - PANEL - first),
            0,
        )
        ar, ai = ref[0], ref[1]
        change = dot3(jnp.concatenate([ar, ai], 1), right)
        inside = (lane >= first) & (lane < first + PANEL)
        ref[0] = jnp.where(inside, 0.0, ar) - change[:, :N]
        ref[1] = jnp.where(inside, 0.0, ai) - change[:, N:]
        ref[0, first : first + PANEL, :] = pr
        ref[1, first : first + PANEL, :] = pi


def rows8_lane(x, lane):
    return jnp.broadcast_to(x[:, lane : lane + 1], (8, N))


def meet(partners):
    barrier = pltpu.get_barrier_semaphore()
    for partner in partners:
        pl.semaphore_signal(barrier, inc=1, device_id=partner, device_id_type=MESH)
    pl.semaphore_wait(barrier, len(partners))


def gather_kernel(ham, coupling, ham4, link5, local, send, recv):
    s, e = lax.axis_index("space"), lax.axis_index("energy")
    y, core = s // 2, s % 2
    nxt, prv = (y + 1) % 4, (y + 3) % 4
    other = (y * 2 + 1 - core, e)
    ahead = [(nxt * 2, e), (nxt * 2 + 1, e)]
    behind = [(prv * 2, e), (prv * 2 + 1, e)]
    meet([other] + ahead + behind)
    base = core * 2
    mine = [
        pltpu.make_async_copy(ham, ham4.at[pl.ds(base, 2)], local.at[0]),
        pltpu.make_async_copy(coupling, link5.at[pl.ds(base + 1, 2)], local.at[1]),
    ]

    def remote(src, dst, i, to):
        return pltpu.make_async_remote_copy(
            src, dst, send.at[i], recv.at[i], device_id=to, device_id_type=MESH
        )

    last = [remote(coupling.at[1], link5.at[0], i, ahead[i]) for i in range(2)]

    @pl.when(core == 1)
    def _():
        last[0].start()
        last[1].start()

    pair = [
        remote(ham, ham4.at[pl.ds(base, 2)], 2, other),
        remote(coupling, link5.at[pl.ds(base + 1, 2)], 3, other),
    ]
    for c in pair + mine:
        c.start()
    for c in pair + mine:
        c.wait()

    @pl.when(core == 1)
    def _():
        last[0].wait_send()
        last[1].wait_send()
        last[1].wait_recv()

    @pl.when(core == 0)
    def _():
        last[0].wait_recv()


def swap_kernel(partner_of, x, out, send, recv):
    s, e = lax.axis_index("space"), lax.axis_index("energy")
    partner = (partner_of(s // 2) * 2 + s % 2, e)
    meet([partner])
    copy = pltpu.make_async_remote_copy(
        x, out, send, recv, device_id=partner, device_id_type=MESH
    )
    copy.start()
    copy.wait()


def energy_kernel(x, out, send, recv):
    s, e = lax.axis_index("space"), lax.axis_index("energy")
    targets = [(s, (e + d) % ENERGIES) for d in (1, ENERGIES - 1, ENERGIES // 2)]
    meet(targets)
    copies = [
        pltpu.make_async_remote_copy(
            x, out.at[i], send.at[i], recv.at[i], device_id=to, device_id_type=MESH
        )
        for i, to in enumerate(targets)
    ]
    for c in copies:
        c.start()
    for c in copies:
        c.wait()


def swap(x, partner_of, identity):
    return pl.pallas_call(
        functools.partial(swap_kernel, partner_of),
        out_shape=jax.ShapeDtypeStruct(x.shape, F32),
        in_specs=[VM],
        out_specs=VM,
        scratch_shapes=[pltpu.SemaphoreType.DMA, pltpu.SemaphoreType.DMA],
        compiler_params=pltpu.CompilerParams(collective_id=identity, has_side_effects=True),
    )(x)


def across_pair(y):
    return y + 1 - 2 * (y % 2)


def across_middle(y):
    return 3 - y


def chain_kernel(ham4, link5, contact, state, parts, s_ref, a_ref, b_ref, h_ref, g_ref, p_ref, q_ref, ef_ref):
    space = lax.axis_index("space")
    y, core = space // 2, space % 2
    right = y >= 2
    outer = (y == 0) | (y == 3)
    inner_core = jnp.where(right, 1 - core, core) == 1
    energy = -2.0 + 4.0 * (lax.axis_index("energy").astype(F32) + 0.5) / ENERGIES
    eye = jnp.where(
        lax.broadcasted_iota(jnp.int32, (N, N), 0) == lax.broadcasted_iota(jnp.int32, (N, N), 1), 1.0, 0.0
    )

    def oriented(index):
        c = get(link5, index)
        return pick(right, adj(c), c)

    for k in range(4):
        h = get(ham4, jnp.where(right, 3 - k, k))
        a_ref[k, 0] = energy * eye - 0.5 * (h[0] + h[0].T)
        a_ref[k, 1] = BROADENING * eye - 0.5 * (h[1] - h[1].T)
    for k in range(3):
        b = oriented(jnp.where(right, 3 - k, k + 1))
        put(b_ref, b, k)
        put(h_ref, adj(b), k)
    ext = oriented(jnp.where(right, 4, 0))
    lead = pick(right, ext, get(contact))
    gamma = mul(lead, adj(lead))
    weight = jnp.where(outer, 0.5, 0.0)
    put(s_ref, (a_ref[0, 0] - weight * gamma[1], a_ref[0, 1] + weight * gamma[0]))
    zero = jnp.zeros((N, N), F32)
    ext = pick(outer, (zero, zero), ext)
    put(ef_ref, ext, 0, 0)
    put(ef_ref, adj(ext), 1, 0)
    put(state, (zero, zero), 3)

    def level(k, _):
        invert(s_ref)
        g = get(s_ref)
        put(g_ref, g, k)
        b, bh = get(b_ref, k), get(h_ref, k)
        p = mul(g, b)
        put(s_ref, sub(get(a_ref, k + 1), mul(bh, p)))
        q = mul(bh, g)
        put(p_ref, p, k)
        put(q_ref, q, k)
        e, f = get(ef_ref, 0, k), get(ef_ref, 1, k)
        put(ef_ref, mul(e, p), 0, k + 1)
        put(ef_ref, mul(q, f), 1, k + 1)
        put(state, add(get(state, 3), mul(mul(e, g), f)), 3)
        return 0

    lax.fori_loop(0, 3, level, 0)
    put(state, get(s_ref), 0)
    put(state, get(ef_ref, 0, 3), 1)
    put(state, get(ef_ref, 1, 3), 2)

    @pl.when(inner_core)
    def _():
        g2 = get(g_ref, 2)
        put(parts, g2, 0, 0)
        put(parts, get(p_ref, 2), 0, 1)
        put(parts, get(q_ref, 2), 0, 2)
        put(parts, mul(g2, get(ef_ref, 1, 2)), 0, 3)
        put(parts, mul(get(ef_ref, 0, 2), g2), 0, 4)
        put(parts, (zero, zero), 1, 0)
        put(parts, (eye, zero), 1, 1)
        put(parts, (eye, zero), 1, 2)
        put(parts, (zero, zero), 1, 3)
        put(parts, (zero, zero), 1, 4)

    @pl.when(jnp.logical_not(inner_core))
    def _():
        p0, p1, q0, q1 = get(p_ref, 0), get(p_ref, 1), get(q_ref, 0), get(q_ref, 1)
        w1 = add(get(g_ref, 1), mul(mul(p1, get(g_ref, 2)), q1))
        l1, r1 = mul(p1, get(p_ref, 2)), mul(get(q_ref, 2), q1)
        put(parts, w1, 0, 0)
        put(parts, l1, 0, 1)
        put(parts, r1, 0, 2)
        put(parts, mul(w1, get(ef_ref, 1, 1)), 0, 3)
        put(parts, mul(get(ef_ref, 0, 1), w1), 0, 4)
        w0 = add(get(g_ref, 0), mul(mul(p0, w1), q0))
        put(parts, w0, 1, 0)
        put(parts, mul(p0, l1), 1, 1)
        put(parts, mul(r1, q0), 1, 2)
        put(parts, mul(w0, get(ef_ref, 1, 0)), 1, 3)
        put(parts, mul(get(ef_ref, 0, 0), w0), 1, 4)


def outer_join_kernel(state, theirs, parts_in, schur, join, parts, s_ref):
    put(s_ref, sub(get(theirs), get(state, 3)))
    invert(s_ref)
    k = get(s_ref)
    e3, f3 = get(state, 1), get(state, 2)
    ke, fk = mul(k, e3), mul(f3, k)
    put(schur, sub(get(state, 0), mul(f3, ke)))
    put(join, k, 0)
    put(join, ke, 1)
    put(join, fk, 2)
    for t in range(2):
        le, re = get(parts_in, t, 3), get(parts_in, t, 4)
        put(parts, add(get(parts_in, t, 0), mul(mul(le, k), re)), t, 0)
        put(parts, add(get(parts_in, t, 1), mul(le, ke)), t, 1)
        put(parts, add(get(parts_in, t, 2), mul(fk, re)), t, 2)


def middle_kernel(schur, theirs, link5, join, green, s_ref):
    right = lax.axis_index("space") // 2 >= 2
    c = get(link5, jnp.where(right, 0, 4))
    b = pick(right, adj(c), c)
    s_ref[...] = theirs[...]

    def level(k, _):
        invert(s_ref)

        @pl.when(k == 0)
        def _():
            put(s_ref, sub(get(schur), mul(mul(b, get(s_ref)), adj(b))))

        return 0

    lax.fori_loop(0, 2, level, 0)
    g = get(s_ref)
    put(green, g, 0)
    put(green, add(get(join, 0), mul(get(join, 1), mul(g, get(join, 2)))), 1)


def close_kernel(green, theirs, parts, out):
    space = lax.axis_index("space")
    y, core = space // 2, space % 2
    outer = (y == 0) | (y == 3)
    right = y >= 2
    inner_core = jnp.where(right, 1 - core, core) == 1
    x = pick(outer, get(theirs), get(green, 0))
    for t in range(2):
        put(
            out,
            add(get(parts, t, 0), mul(mul(get(parts, t, 1), x), get(parts, t, 2))),
            jnp.where(jnp.where(right, inner_core, jnp.logical_not(inner_core)), 1 - t, t),
        )


def call(kernel, outs, scratch, *args):
    return pl.pallas_call(
        kernel,
        out_shape=[jax.ShapeDtypeStruct(o, F32) for o in outs],
        in_specs=[VM] * len(args),
        out_specs=[VM] * len(outs),
        scratch_shapes=[pltpu.VMEM(s, F32) for s in scratch],
        compiler_params=pltpu.CompilerParams(vmem_limit_bytes=48 << 20),
    )(*args)


def on_device(ham_diag, coupling, contact_left, mode_weight, mode_offset, pattern):
    ham4, link5 = pl.pallas_call(
        gather_kernel,
        out_shape=[jax.ShapeDtypeStruct((4,) + BLOCK, F32), jax.ShapeDtypeStruct((5,) + BLOCK, F32)],
        in_specs=[VM] * 2,
        out_specs=[VM] * 2,
        scratch_shapes=[
            pltpu.SemaphoreType.DMA((2,)),
            pltpu.SemaphoreType.DMA((4,)),
            pltpu.SemaphoreType.DMA((4,)),
        ],
        compiler_params=pltpu.CompilerParams(collective_id=0, has_side_effects=True),
    )(ham_diag, coupling)
    state, parts = call(
        chain_kernel,
        [(4,) + BLOCK, (2, 5) + BLOCK],
        [BLOCK, (4,) + BLOCK, (3,) + BLOCK, (3,) + BLOCK, (3,) + BLOCK, (3,) + BLOCK, (3,) + BLOCK, (2, 4) + BLOCK],
        ham4,
        link5,
        contact_left,
    )
    theirs = swap(state[0], across_pair, 1)
    schur, join, parts = call(
        outer_join_kernel, [BLOCK, (3,) + BLOCK, (2, 3) + BLOCK], [BLOCK], state, theirs, parts
    )
    theirs = swap(schur, across_middle, 2)
    (green,) = call(middle_kernel, [(2,) + BLOCK], [BLOCK], schur, theirs, link5, join)
    theirs = swap(green[1], across_pair, 3)
    (diag,) = call(close_kernel, [(2,) + BLOCK], [], green, theirs, parts)
    got = pl.pallas_call(
        energy_kernel,
        out_shape=jax.ShapeDtypeStruct((3, 2) + BLOCK, F32),
        in_specs=[VM],
        out_specs=VM,
        scratch_shapes=[pltpu.SemaphoreType.DMA((3,)), pltpu.SemaphoreType.DMA((3,))],
        compiler_params=pltpu.CompilerParams(collective_id=4, has_side_effects=True),
    )(diag)
    e = lax.axis_index("energy")
    source = jnp.stack([e - 1, e + 1, jnp.where(e >= ENERGIES // 2, e - ENERGIES // 2, e + ENERGIES // 2)])
    hits = (source[:, None] == e - mode_offset[None, :]) & ((source >= 0) & (source < ENERGIES))[:, None]
    weight = jnp.sum(jnp.where(hits, mode_weight[None, :], 0.0), 1)
    total = got[0] * weight[0] + got[1] * weight[1] + got[2] * weight[2]
    return (total * pattern.astype(F32))[None]


def solution(mesh):
    placed = (P("space", None, None, None), P("space", None, None, None), P(), P(), P(), P())
    return jax.shard_map(
        on_device,
        mesh=mesh,
        in_specs=placed,
        out_specs=P("energy", "space", None, None, None),
        check_vma=False,
    )
```

time: 1550 us -> 112 us (0.07)
  other arithmetic: 1000 us -> 3.98 us
  waiting for transfers between devices: 183 us -> 0 us
  matrix products: 133 us -> 0 us
  local copies, waits for them, and re-layouts: 143 us -> 11.7 us
  Pallas kernels: 0 us -> 93.9 us
  loops' own time: 44.2 us -> 0 us
  between operations: 20.7 us -> 0.18 us
    another operation x194 -> x0, other arithmetic: 980 us -> none  [the longest x125 624 us: invert(): factor = jnp.linalg.cholesky(normal)]
    all_gather x5 -> x0, waiting for transfers between devices: 104 us -> none  [carried_in(): pieces = jax.tree.map(lambda part: lax.all_gather(part, axis), value)]
    dot_general x183 -> x0, matrix products: 96.5 us -> none  [the longest x165 89.1 us: product(): joined = jnp.dot(real_form_of(former), stacked, precision=HIGHEST)]
    pallas_call x0 -> x9, Pallas kernels: none -> 93.9 us  [the longest x4 47.9 us: call(): pl.pallas_call(kernel, out_shape=[jax.ShapeDtypeStruct(o, F32) for o in o...]
    unnamed x7 -> x0, waiting for transfers between devices: 79 us -> none
    another operation x178 -> x0, local copies, waits for them, and re-layouts: 75.8 us -> none  [the longest x127 72.6 us: invert(): jax.scipy.linalg.cho_solve((factor, True), real_form.T[:, :order_size])]
    another operation x20 -> x0, loops' own time: 44.2 us -> none  [the longest x2 43.3 us: carried_in(): return lax.fori_loop(0, count - 1, lap, subtotal)]
    another operation x144 -> x0, matrix products: 36.8 us -> none  [the longest x108 27.7 us: invert(): jax.scipy.linalg.cho_solve((factor, True), real_form.T[:, :order_size])]
  transfers between devices with their start and end apart: 6 -> 0, of which waited for: 6 -> 0; matrix products, arithmetic and copies ran while one was open for 0% -> 0% of each run, Pallas kernels for 0% -> 0%
where the time goes in v1:
time: 112 us; the launch traced here: 110 us
  Pallas kernels  93.9 us (84%)
  local copies, waits for them, and re-layouts  11.7 us (10%)
  other arithmetic  3.98 us (4%)
    pallas_call x4, Pallas kernels, call(): pl.pallas_call(kernel, out_shape=[jax.ShapeDtypeStruct(o, F32) for o in o...  47.9 us
    pallas_call x3, Pallas kernels, swap(): pl.pallas_call(functools.partial(swap_kernel, partner_of), out_shape=jax....  21.1 us
    pallas_call x1, Pallas kernels, on_device(): pl.pallas_call(energy_kernel, out_shape=jax.ShapeDtypeStruct((3, 2) + BLO...  16.6 us
    unnamed x30, local copies, waits for them, and re-layouts  9.76 us
    pallas_call x1, Pallas kernels, on_device(): pl.pallas_call(gather_kernel, out_shape=[jax.ShapeDtypeStruct((4,) + BLOC...  8.39 us
    mul x1, other arithmetic, on_device(): return (total * pattern.astype(F32))[None]  3.7 us

profile of v1, /device:TPU:0, one launch (start us, length us, event | category | flops | bytes accessed | tf_op | source)
XLA Modules:
  0.0 109.8 jit_solution(2865089900914232763)
XLA Ops:
  0.0 8.4 %shard_map.64 = (f32[4,2,128,128]{3,2,1,0:T(8,128)}, f32[5,2,128,128]{3,2,1,0:T(8,128)}) custom-call(f32[2,2,128,128]{3,2,1,0:T(8,128)} %ham.1, f32[2,2,128,128]{3,2,1,0:T(8,128)} %coupling.1), custom_call_target="tpu_custom_call" | custom-call | tf_op jit(solution)/shard_map/pallas_call | solution.py:398
  8.4 0.0 copy-start
  8.4 1.1 copy-done
  9.5 0.0 copy-start.6
  9.5 1.0 copy-done.6
  10.5 0.0 copy-start.11
  10.5 0.9 copy-done.11
  11.4 25.3 %shard_map.65 = (f32[4,2,128,128]{3,2,1,0:T(8,128)S(1)}, f32[2,5,2,128,128]{4,3,2,1,0:T(8,128)S(1)}) custom-call(f32[4,2,128,128]{3,2,1,0:T(8,128)S(1)} %copy-done.6, f32[5,2,128,128]{3,2,1,0:T(8,128)S(1)} %copy-done, f32[2,128,128]{2,1,0:T(8,128)S(1)} %copy-done.11), custom_call_target="tpu_custom_call" | custom-call | tf_op jit(solution)/shard_map/pallas_call | solution.py:387
  36.7 0.7 slice_bitcast_fusion.1.x
  37.4 0.0 copy-start.1
  37.4 6.8 %shard_map.66.theirs = f32[2,128,128]{2,1,0:T(8,128)} custom-call(f32[2,128,128]{2,1,0:T(8,128)} %slice_bitcast_fusion.1.x), custom_call_target="tpu_custom_call" | custom-call | tf_op jit(solution)/shard_map/pallas_call | solution.py:228
  44.2 0.0 copy-start.8
  44.2 0.9 copy-done.8
  45.1 7.6 %shard_map.67 = (f32[2,128,128]{2,1,0:T(8,128)S(1)}, f32[3,2,128,128]{3,2,1,0:T(8,128)S(1)}, f32[2,3,2,128,128]{4,3,2,1,0:T(8,128)S(1)}) custom-call(f32[4,2,128,128]{3,2,1,0:T(8,128)S(1)} %get-tuple-element.14.state, f32[2,128,128]{2,1,0:T(8,128)S(1)} %copy-done.8, f32[2,5,2,128,128]{4,3,2,1,0:T(8,128)S(1)} %get-tuple-element.15.parts_in), custom_call_target="tpu_custom_call" | custom-call | tf_op jit(solution)/shard_map/pallas_call | solution.py:387
  52.8 0.0 copy-start.3
  52.8 0.6 copy-done.3
  53.4 0.0 copy-start.9
  53.4 0.8 copy-done.9
  54.2 7.7 %shard_map.68.theirs = f32[2,128,128]{2,1,0:T(8,128)} custom-call(f32[2,128,128]{2,1,0:T(8,128)} %copy-done.3), custom_call_target="tpu_custom_call" | custom-call | tf_op jit(solution)/shard_map/pallas_call | solution.py:228
  61.9 0.0 copy-done.1
  62.0 0.0 copy-start.4
  62.0 0.9 copy-done.4
  62.9 0.0 copy-start.5
  62.9 0.9 copy-done.5
  63.8 0.0 copy-start.10
  63.8 1.0 copy-done.10
  64.8 14.1 %shard_map.69.green = f32[2,2,128,128]{3,2,1,0:T(8,128)S(1)} custom-call(f32[2,128,128]{2,1,0:T(8,128)S(1)} %copy-done.4, f32[2,128,128]{2,1,0:T(8,128)S(1)} %copy-done.5, f32[5,2,128,128]{3,2,1,0:T(8,128)S(1)} %copy-done.1, f32[3,2,128,128]{3,2,1,0:T(8,128)S(1)} %copy-done.10), custom_call_target="tpu_custom_call" | custom-call | tf_op jit(solution)/shard_map/pallas_call | solution.py:387
  78.9 0.7 slice_bitcast_fusion.x
  79.5 6.5 %shard_map.70.theirs = f32[2,128,128]{2,1,0:T(8,128)} custom-call(f32[2,128,128]{2,1,0:T(8,128)} %slice_bitcast_fusion.x), custom_call_target="tpu_custom_call" | custom-call | tf_op jit(solution)/shard_map/pallas_call | solution.py:228
  86.1 0.0 copy-start.14
  86.1 0.0 copy-start.13
  86.1 0.0 copy-start.7
  86.1 0.9 copy-done.7
  87.0 0.0 copy-start.12
  87.0 0.9 shard_map.71.x
  87.9 0.0 copy-start.2
  87.9 0.7 copy-done.2
  88.6 16.6 %shard_map.72 = f32[3,2,2,128,128]{4,3,2,1,0:T(8,128)} custom-call(f32[2,2,128,128]{3,2,1,0:T(8,128)} %copy-done.2), custom_call_target="tpu_custom_call" | custom-call | tf_op jit(solution)/shard_map/pallas_call | solution.py:426
  105.2 0.1 compare_and_fusion
  105.3 0.0 copy-done.14
  105.3 0.0 copy-done.13
  105.3 0.2 select_reduce_fusion
  105.5 0.7 fusion
  106.1 0.0 copy-done.12
  106.1 3.7 %add_multiply_fusion = f32[1,2,2,128,128]{4,3,2,1,0:T(8,128)} fusion(f32[3,2,2,128,128]{4,3,2,1,0:T(8,128)} %shard_map.72, f32[128,128]{1,0:T(8,128)S(1)} %convert_element_type.3, f32[]{:T(128)} %bitcast.7, f32[]{:T(128)} %bitcast.6, f32[]{:T(128)} %bitcast.5), kind=kLoop, calls=%fused_computation | loop fusion | flops 393216 | bytes 1114124 | tf_op jit(solution)/shard_map/mul | solution.py:439
  (2 shorter events, 0.0 us)
Async XLA Ops:
  8.4 1.1 copy-start
  9.5 1.0 copy-start.6
  10.5 0.9 copy-start.11
  37.4 24.6 %copy-start.1 = (f32[5,2,128,128]{3,2,1,0:T(8,128)S(1)}, f32[5,2,128,128]{3,2,1,0:T(8,128)}, u32[]{:S(2)}) copy-start(f32[5,2,128,128]{3,2,1,0:T(8,128)} %get-tuple-element.13.link5) | copy-start | bytes 1966084
  44.2 0.9 copy-start.8
  52.8 0.7 copy-start.3
  53.4 0.8 copy-start.9
  62.0 0.9 copy-start.4
  62.9 0.9 copy-start.5
  63.8 1.0 copy-start.10
  86.1 19.2 %copy-start.14 = (s32[4]{0:T(128)S(1)}, s32[4]{0:T(128)}, u32[]{:S(2)}) copy-start(s32[4]{0:T(128)} %param.10) | copy-start | bytes 52
  86.1 19.2 %copy-start.13 = (f32[4]{0:T(128)S(1)}, f32[4]{0:T(128)}, u32[]{:S(2)}) copy-start(f32[4]{0:T(128)} %param.9) | copy-start | bytes 52
  86.1 0.9 copy-start.7
  87.0 19.1 %copy-start.12 = (s32[128,128]{1,0:T(8,128)S(1)}, s32[128,128]{1,0:T(8,128)}, u32[]{:S(2)}) copy-start(s32[128,128]{1,0:T(8,128)} %param.11) | copy-start | bytes 196612
  87.9 0.7 copy-start.2

commit v2 on v0

v2 whole, which is shorter than its diff:
```python
import functools

import jax
import jax.numpy as jnp
from jax import lax
from jax.experimental import pallas as pl
from jax.experimental.pallas import tpu as pltpu
from jax.sharding import PartitionSpec as P

N = 128
PANEL = 16
ENERGIES = 16
BROADENING = 0.1
F32 = jnp.float32
MESH = pl.DeviceIdType.MESH
VM = pl.BlockSpec(memory_space=pltpu.VMEM)
SM = pl.BlockSpec(memory_space=pltpu.SMEM)
HIGHEST = lax.Precision.HIGHEST
BLOCK = (2, N, N)
STEPS = (1, ENERGIES - 1, ENERGIES // 2)


def split(x):
    high = x.astype(jnp.bfloat16)
    return high, (x - high.astype(F32)).astype(jnp.bfloat16)


def dot3(a, b):
    ah, al = split(a)
    bh, bl = split(b)
    d = functools.partial(jnp.dot, preferred_element_type=F32)
    return d(ah, bh) + (d(al, bh) + d(ah, bl))


def dot6(a, b):
    return jnp.dot(a, b, precision=HIGHEST, preferred_element_type=F32)


def mul(a, b, dot=dot6):
    left = jnp.concatenate([a[0], a[1]], 1)
    right = jnp.concatenate(
        [jnp.concatenate([b[0], b[1]], 1), jnp.concatenate([-b[1], b[0]], 1)], 0
    )
    out = dot(left, right)
    return out[:, :N], out[:, N:]


def add(a, b):
    return a[0] + b[0], a[1] + b[1]


def sub(a, b):
    return a[0] - b[0], a[1] - b[1]


def adj(a):
    return a[0].T, -a[1].T


def pick(cond, a, b):
    return jnp.where(cond, a[0], b[0]), jnp.where(cond, a[1], b[1])


def get(ref, *index):
    return ref[index + (0,)], ref[index + (1,)]


def put(ref, value, *index):
    ref[index + (0,)] = value[0]
    ref[index + (1,)] = value[1]


def spread(x, rows):
    return jnp.broadcast_to(x, (rows, N))


def eliminate(rr, ri, first):
    b, groups = PANEL, PANEL // 8
    lane = lax.broadcasted_iota(jnp.int32, (b, N), 1)
    row = lax.broadcasted_iota(jnp.int32, (b, N), 0)
    for g in range(groups):
        c0 = first + 8 * g
        here = (lane >= c0) & (lane < c0 + 8)
        unit = jnp.where(lane - first == row, 1.0, 0.0)
        xr = jnp.stack([spread(rr[:, c0 + j : c0 + j + 1], b) for j in range(8)] + [jnp.where(here, unit, rr)])
        xi = jnp.stack([spread(ri[:, c0 + j : c0 + j + 1], b) for j in range(8)] + [jnp.where(here, 0.0, ri)])
        for k in range(8):
            t = 8 * g + k
            dr, di = xr[0], xi[0]
            xr, xi = xr[1:], xi[1:]
            pr, pi = spread(dr[t : t + 1], 8), spread(di[t : t + 1], 8)
            inv = 1.0 / (pr * pr + pi * pi)
            qr, qi = (pr * inv)[None], (-pi * inv)[None]
            shape = (8 - k, 8, N)
            ar = jnp.broadcast_to(xr[:, t : t + 1, :], shape)
            ai = jnp.broadcast_to(xi[:, t : t + 1, :], shape)
            sr, si = qr * ar - qi * ai, qr * ai + qi * ar
            outr, outi = [], []
            for v in range(groups):
                s = slice(8 * v, 8 * v + 8)
                yr = xr[:, s] - dr[None, s] * sr + di[None, s] * si
                yi = xi[:, s] - dr[None, s] * si - di[None, s] * sr
                if v == g:
                    at_pivot = (row[:8] == k)[None]
                    yr, yi = jnp.where(at_pivot, sr, yr), jnp.where(at_pivot, si, yi)
                outr.append(yr)
                outi.append(yi)
            xr, xi = jnp.concatenate(outr, 1), jnp.concatenate(outi, 1)
        rr, ri = xr[0], xi[0]
    return rr, ri


def inverse(a):
    ar, ai = a
    b = PANEL
    lane = lax.broadcasted_iota(jnp.int32, (N, N), 1)
    d = functools.partial(jnp.dot, preferred_element_type=F32)
    ahead = (ar[:b], ai[:b])
    for f in range(0, N, b):
        pr, pi = eliminate(*ahead, f)
        inside = (lane >= f) & (lane < f + b)
        zr, zi = jnp.where(inside, 0.0, ar), jnp.where(inside, 0.0, ai)
        ahead = None
        n0 = f + b
        if n0 < N:
            yr, yi = zr[n0 : n0 + b], zi[n0 : n0 + b]
            for k in range(b):
                cr = spread(ar[n0 : n0 + b, f + k : f + k + 1], b)
                ci = spread(ai[n0 : n0 + b, f + k : f + k + 1], b)
                sr, si = spread(pr[k : k + 1], b), spread(pi[k : k + 1], b)
                yr, yi = yr - cr * sr + ci * si, yi - cr * si - ci * sr
            ahead = (yr, yi)
        lh, ll = split(jnp.concatenate([ar, ai], 1))
        prh, prl = split(pr)
        pih, pil = split(pi)

        def gap(rows):
            return [jnp.zeros((rows, 2 * N), jnp.bfloat16)] if rows else []

        def right(xr, xi):
            return jnp.concatenate(
                gap(f)
                + [jnp.concatenate([xr, xi], 1)]
                + gap(N - b)
                + [jnp.concatenate([-xi, xr], 1)]
                + gap(N - b - f),
                0,
            )

        rh, rl = right(prh, pih), right(prl, pil)
        change = d(lh, rh) + (d(ll, rh) + d(lh, rl))

        def rows(z, ch, panel, following):
            new = z - ch
            blocks = [new[:f], panel] + ([new[n0:]] if following is None else [following, new[n0 + b :]])
            return jnp.concatenate([x for x in blocks if x.shape[0]], 0)

        ar = rows(zr, change[:, :N], pr, None if ahead is None else ahead[0])
        ai = rows(zi, change[:, N:], pi, None if ahead is None else ahead[1])
    return ar, ai


def kernel(
    ham, coupling, contact, pattern, mode_weight, mode_offset, out,
    ham_in, link_in, last_in, s_ref, a_ref, b_ref, h_ref, g_ref, p_ref, q_ref, e_ref, f_ref, u_ref,
    part, schur, schur_in, join, x_ref, gee, diag, got, send, recv, esend, erecv,
):
    space, me = lax.axis_index("space"), lax.axis_index("energy")
    y, core = space // 2, space % 2
    right = y >= 2
    outer = (y == 0) | (y == 3)
    inner = jnp.logical_not(outer)
    inner_core = jnp.where(right, 1 - core, core) == 1
    nxt, prv = (y + 1) % 4, (y + 3) % 4
    other = (y * 2 + 1 - core, me)
    ahead = [(nxt * 2, me), (nxt * 2 + 1, me)]
    behind = [(prv * 2, me), (prv * 2 + 1, me)]
    pair = ((y + 1 - 2 * (y % 2)) * 2 + core, me)
    middle = ((3 - y) * 2 + core, me)
    targets = [(space, (me + d) % ENERGIES) for d in STEPS]

    def remote(src, dst, i, to):
        return pltpu.make_async_remote_copy(
            src, dst, send.at[i], recv.at[i], device_id=to, device_id_type=MESH
        )

    barrier = pltpu.get_barrier_semaphore()
    for partner in [other] + ahead + behind + targets:
        pl.semaphore_signal(barrier, inc=1, device_id=partner, device_id_type=MESH)
    pl.semaphore_wait(barrier, 8)

    send_ham = remote(ham, ham_in, 0, other)
    send_link = remote(coupling, link_in, 1, other)
    last = [remote(coupling.at[1], last_in, 2 + i, ahead[i]) for i in range(2)]
    send_ham.start()
    send_link.start()

    @pl.when(core == 1)
    def _():
        last[0].start()
        last[1].start()

    energy = -2.0 + 4.0 * (me.astype(F32) + 0.5) / ENERGIES
    eye = jnp.where(
        lax.broadcasted_iota(jnp.int32, (N, N), 0) == lax.broadcasted_iota(jnp.int32, (N, N), 1), 1.0, 0.0
    )
    zero = jnp.zeros((N, N), F32)

    def place_block(ref, i, b):
        k = jnp.where(right, 3 - b, b)
        h = get(ref, i)
        a_ref[k, 0] = energy * eye - 0.5 * (h[0] + h[0].T)
        a_ref[k, 1] = BROADENING * eye - 0.5 * (h[1] - h[1].T)

    def place_link(value, slot):
        turned = adj(value)
        put(b_ref, pick(right, turned, value), slot)
        put(h_ref, pick(right, value, turned), slot)

    def link_slot(b):
        return jnp.where(right, jnp.where(b == 3, 4, 2 - b), b)

    for i in range(2):
        place_block(ham, i, core * 2 + i)
        place_link(get(coupling, i), link_slot(core * 2 + i))
    send_ham.wait()
    for i in range(2):
        place_block(ham_in, i, (1 - core) * 2 + i)
    send_link.wait()
    for i in range(2):
        place_link(get(link_in, i), link_slot((1 - core) * 2 + i))

    @pl.when(core == 1)
    def _():
        last[0].wait_send()
        last[1].wait_send()
        last[1].wait_recv()

    @pl.when(core == 0)
    def _():
        last[0].wait_recv()

    place_link(get(last_in), jnp.where(right, 3, 4))
    lead, lead_adj = get(b_ref, 4), get(h_ref, 4)
    own = get(contact)
    gamma = mul(pick(right, lead, own), pick(right, lead_adj, adj(own)))
    weight = jnp.where(outer, 0.5, 0.0)
    put(s_ref, (a_ref[0, 0] - weight * gamma[1], a_ref[0, 1] + weight * gamma[0]))
    put(e_ref, pick(outer, (zero, zero), lead), 0)
    put(f_ref, pick(outer, (zero, zero), lead_adj), 0)
    put(u_ref, (zero, zero))

    send_schur = remote(schur.at[0], schur_in.at[0], 4, pair)
    send_middle = remote(schur.at[1], schur_in.at[1], 5, middle)
    send_green = remote(gee, x_ref, 6, pair)

    def level(k, _):
        g = inverse(get(s_ref))

        @pl.when(k < 3)
        def _():
            put(g_ref, g, k)
            p = mul(g, get(b_ref, k))
            new = sub(get(a_ref, k + 1), mul(get(h_ref, k), p))
            put(s_ref, new)

            @pl.when(k == 2)
            def _():
                put(schur, new, 0)
                send_schur.start()

            q = mul(get(h_ref, k), g, dot3)
            put(p_ref, p, k)
            put(q_ref, q, k)
            e, f = get(e_ref, k), get(f_ref, k)
            put(e_ref, mul(e, p, dot3), k + 1)
            put(f_ref, mul(q, f, dot3), k + 1)
            put(u_ref, add(get(u_ref), mul(mul(e, g, dot3), f, dot3)))

        @pl.when((k == 2) & inner_core)
        def _():
            g2 = get(g_ref, 2)
            put(part, g2, 0, 0)
            put(part, get(p_ref, 2), 0, 1)
            put(part, get(q_ref, 2), 0, 2)
            put(part, mul(g2, get(f_ref, 2), dot3), 0, 3)
            put(part, mul(get(e_ref, 2), g2, dot3), 0, 4)
            put(part, (zero, zero), 1, 0)
            put(part, (eye, zero), 1, 1)
            put(part, (eye, zero), 1, 2)
            put(part, (zero, zero), 1, 3)
            put(part, (zero, zero), 1, 4)

        @pl.when((k == 2) & jnp.logical_not(inner_core))
        def _():
            p0, p1, q0, q1 = get(p_ref, 0), get(p_ref, 1), get(q_ref, 0), get(q_ref, 1)
            w1 = add(get(g_ref, 1), mul(mul(p1, get(g_ref, 2), dot3), q1, dot3))
            l1, r1 = mul(p1, get(p_ref, 2), dot3), mul(get(q_ref, 2), q1, dot3)
            put(part, w1, 0, 0)
            put(part, l1, 0, 1)
            put(part, r1, 0, 2)
            put(part, mul(w1, get(f_ref, 1), dot3), 0, 3)
            put(part, mul(get(e_ref, 1), w1, dot3), 0, 4)
            w0 = add(get(g_ref, 0), mul(mul(p0, w1, dot3), q0, dot3))
            put(part, w0, 1, 0)
            put(part, mul(p0, l1, dot3), 1, 1)
            put(part, mul(r1, q0, dot3), 1, 2)
            put(part, mul(w0, get(f_ref, 0), dot3), 1, 3)
            put(part, mul(get(e_ref, 0), w0, dot3), 1, 4)

        @pl.when(k == 2)
        def _():
            send_schur.wait()
            put(s_ref, sub(get(schur_in, 0), get(u_ref)))

        @pl.when(k == 3)
        def _():
            e3, f3 = get(e_ref, 3), get(f_ref, 3)
            ke = mul(g, e3)
            put(schur, sub(get(schur, 0), mul(f3, ke)), 1)
            send_middle.start()
            fk = mul(f3, g, dot3)
            put(join, g, 0)
            put(join, ke, 1)
            put(join, fk, 2)
            for t in range(2):
                le, re = get(part, t, 3), get(part, t, 4)
                put(part, add(get(part, t, 0), mul(mul(le, g, dot3), re, dot3)), t, 0)
                put(part, add(get(part, t, 1), mul(le, ke, dot3)), t, 1)
                put(part, add(get(part, t, 2), mul(fk, re, dot3)), t, 2)
            send_middle.wait()
            s_ref[...] = schur_in[1]

        @pl.when(k == 4)
        def _():
            put(s_ref, sub(get(schur, 1), mul(mul(get(b_ref, 3), g), get(h_ref, 3))))

        @pl.when((k == 5) & inner)
        def _():
            put(gee, add(get(join, 0), mul(get(join, 1), mul(g, get(join, 2)))))
            send_green.start()
            put(x_ref, g)

        return 0

    lax.fori_loop(0, 6, level, 0)

    @pl.when(outer)
    def _():
        send_green.wait_recv()

    x = get(x_ref)
    copies = []
    for t in range(2):
        put(diag, add(get(part, t, 0), mul(mul(get(part, t, 1), x), get(part, t, 2))), t)
        for i, to in enumerate(targets):
            copy = pltpu.make_async_remote_copy(
                diag.at[t], got.at[i, t], esend.at[i, t], erecv.at[i, t], device_id=to, device_id_type=MESH
            )
            copy.start()
            copies.append(copy)

    @pl.when(inner)
    def _():
        send_green.wait_send()

    half = ENERGIES // 2
    shifts = [
        (jnp.where(me >= 1, 1, 99)),
        (jnp.where(me <= ENERGIES - 2, -1, 99)),
        (jnp.where(me >= half, half, -half)),
    ]
    weights = []
    for shift in shifts:
        w = jnp.float32(0.0)
        for m in range(4):
            w = w + jnp.where(mode_offset[m] == shift, mode_weight[m], 0.0)
        weights.append(w)
    mask = pattern[...].astype(F32)
    first = jnp.where(right, inner_core, jnp.logical_not(inner_core)).astype(jnp.int32)
    for t in range(2):
        for i in range(3):
            copies[3 * t + i].wait()
        slot = first if t == 0 else 1 - first
        for c in range(2):
            total = got[0, t, c] * weights[0] + got[1, t, c] * weights[1] + got[2, t, c] * weights[2]
            out[0, slot, c] = total * mask


def on_device(ham_diag, coupling, contact_left, mode_weight, mode_offset, pattern):
    blocks = [(2,), (2,), (), (), (4,), (5,), (5,), (3,), (3,), (3,), (4,), (4,), ()]
    blocks += [(2, 5), (2,), (2,), (3,), (), (), (2,), (3, 2)]
    return pl.pallas_call(
        kernel,
        out_shape=jax.ShapeDtypeStruct((1, 2) + BLOCK, F32),
        in_specs=[VM, VM, VM, VM, SM, SM],
        out_specs=VM,
        scratch_shapes=[pltpu.VMEM(b + BLOCK, F32) for b in blocks]
        + [
            pltpu.SemaphoreType.DMA((7,)),
            pltpu.SemaphoreType.DMA((7,)),
            pltpu.SemaphoreType.DMA((3, 2)),
            pltpu.SemaphoreType.DMA((3, 2)),
        ],
        compiler_params=pltpu.CompilerParams(
            collective_id=0, has_side_effects=True, vmem_limit_bytes=48 << 20
        ),
    )(ham_diag, coupling, contact_left, pattern, mode_weight, mode_offset)


def solution(mesh):
    placed = (P("space", None, None, None), P("space", None, None, None), P(), P(), P(), P())
    return jax.shard_map(
        on_device,
        mesh=mesh,
        in_specs=placed,
        out_specs=P("energy", "space", None, None, None),
        check_vma=False,
    )
```

time: 1550 us -> 76.3 us (0.05)
  other arithmetic: 1000 us -> 0 us
  waiting for transfers between devices: 183 us -> 0 us
  local copies, waits for them, and re-layouts: 143 us -> 5.66 us
  matrix products: 133 us -> 0 us
  Pallas kernels: 0 us -> 70.1 us
  loops' own time: 44.2 us -> 0 us
  between operations: 20.7 us -> 0.02 us
    another operation x194 -> x0, other arithmetic: 980 us -> none  [the longest x125 624 us: invert(): factor = jnp.linalg.cholesky(normal)]
    all_gather x5 -> x0, waiting for transfers between devices: 104 us -> none  [carried_in(): pieces = jax.tree.map(lambda part: lax.all_gather(part, axis), value)]
    dot_general x183 -> x0, matrix products: 96.5 us -> none  [the longest x165 89.1 us: product(): joined = jnp.dot(real_form_of(former), stacked, precision=HIGHEST)]
    unnamed x7 -> x0, waiting for transfers between devices: 79 us -> none
    another operation x178 -> x0, local copies, waits for them, and re-layouts: 75.8 us -> none  [the longest x127 72.6 us: invert(): jax.scipy.linalg.cho_solve((factor, True), real_form.T[:, :order_size])]
    pallas_call x0 -> x1, Pallas kernels: none -> 70.1 us  [on_device(): pl.pallas_call(kernel, out_shape=jax.ShapeDtypeStruct((1, 2) + BLOCK, F32...]
    another operation x20 -> x0, loops' own time: 44.2 us -> none  [the longest x2 43.3 us: carried_in(): return lax.fori_loop(0, count - 1, lap, subtotal)]
    another operation x144 -> x0, matrix products: 36.8 us -> none  [the longest x108 27.7 us: invert(): jax.scipy.linalg.cho_solve((factor, True), real_form.T[:, :order_size])]
  transfers between devices with their start and end apart: 6 -> 0, of which waited for: 6 -> 0; matrix products, arithmetic and copies ran while one was open for 0% -> 0% of each run, Pallas kernels for 0% -> 0%
where the time goes in v2:
time: 76.3 us; the launch traced here: 75.7 us
  Pallas kernels  70.1 us (92%)
  local copies, waits for them, and re-layouts  5.66 us (7%)
    pallas_call x1, Pallas kernels, on_device(): pl.pallas_call(kernel, out_shape=jax.ShapeDtypeStruct((1, 2) + BLOCK, F32...  70.1 us
    unnamed x13, local copies, waits for them, and re-layouts  5.66 us

profile of v2, /device:TPU:0, one launch (start us, length us, event | category | flops | bytes accessed | tf_op | source)
XLA Modules:
  0.0 75.7 jit_solution(15311965460018574939)
XLA Ops:
  0.0 0.0 copy-start
  0.0 0.9 %copy-done = f32[2,2,128,128]{3,2,1,0:T(8,128)S(1)} copy-done((f32[2,2,128,128]{3,2,1,0:T(8,128)S(1)}, f32[2,2,128,128]{3,2,1,0:T(8,128)}, u32[]{:S(2)}) %copy-start) | copy-done | bytes 262168
  1.0 0.0 copy-start.1
  1.0 0.9 %copy-done.1 = f32[2,2,128,128]{3,2,1,0:T(8,128)S(1)} copy-done((f32[2,2,128,128]{3,2,1,0:T(8,128)S(1)}, f32[2,2,128,128]{3,2,1,0:T(8,128)}, u32[]{:S(2)}) %copy-start.1) | copy-done | bytes 262168
  1.9 0.0 copy-start.2
  1.9 0.9 %copy-done.2 = f32[2,128,128]{2,1,0:T(8,128)S(1)} copy-done((f32[2,128,128]{2,1,0:T(8,128)S(1)}, f32[2,128,128]{2,1,0:T(8,128)}, u32[]{:S(2)}) %copy-start.2) | copy-done | bytes 131096
  2.8 0.0 copy-start.3
  2.8 0.8 %copy-done.3 = s32[128,128]{1,0:T(8,128)S(1)} copy-done((s32[128,128]{1,0:T(8,128)S(1)}, s32[128,128]{1,0:T(8,128)}, u32[]{:S(2)}) %copy-start.3) | copy-done | bytes 65560
  3.6 0.0 copy-start.4
  3.6 0.7 copy-done.4
  4.3 0.0 copy-start.5
  4.3 0.7 copy-done.5
  5.0 70.1 %shard_map.64 = f32[1,2,2,128,128]{4,3,2,1,0:T(8,128)S(1)} custom-call(f32[2,2,128,128]{3,2,1,0:T(8,128)S(1)} %copy-done, f32[2,2,128,128]{3,2,1,0:T(8,128)S(1)} %copy-done.1, f32[2,128,128]{2,1,0:T(8,128)S(1)} %copy-done.2, s32[128,128]{1,0:T(8,128)S(1)} %copy-done.3, f32[4]{0:T(128)S(1)} %copy-done.4, s32[4]{0:T(128)S(1)} %copy-done.5), custom_call_target="tpu_custom_call" | custom-call | tf_op jit(solution)/shard_map/pallas_call | solution.py:393
  75.0 0.7 copy.8
Async XLA Ops:
  0.0 0.9 %copy-start = (f32[2,2,128,128]{3,2,1,0:T(8,128)S(1)}, f32[2,2,128,128]{3,2,1,0:T(8,128)}, u32[]{:S(2)}) copy-start(f32[2,2,128,128]{3,2,1,0:T(8,128)} %ham.1) | copy-start | bytes 786436
  1.0 0.9 %copy-start.1 = (f32[2,2,128,128]{3,2,1,0:T(8,128)S(1)}, f32[2,2,128,128]{3,2,1,0:T(8,128)}, u32[]{:S(2)}) copy-start(f32[2,2,128,128]{3,2,1,0:T(8,128)} %coupling.1) | copy-start | bytes 786436
  1.9 0.9 %copy-start.2 = (f32[2,128,128]{2,1,0:T(8,128)S(1)}, f32[2,128,128]{2,1,0:T(8,128)}, u32[]{:S(2)}) copy-start(f32[2,128,128]{2,1,0:T(8,128)} %contact.1) | copy-start | bytes 393220
  2.8 0.8 %copy-start.3 = (s32[128,128]{1,0:T(8,128)S(1)}, s32[128,128]{1,0:T(8,128)}, u32[]{:S(2)}) copy-start(s32[128,128]{1,0:T(8,128)} %pattern.1) | copy-start | bytes 196612
  3.6 0.7 copy-start.4
  4.3 0.7 copy-start.5

commit v3 on v2

--- a/solution.py
+++ b/solution.py
@@ -14,7 +14,7 @@
 F32 = jnp.float32
 MESH = pl.DeviceIdType.MESH
 VM = pl.BlockSpec(memory_space=pltpu.VMEM)
-SM = pl.BlockSpec(memory_space=pltpu.SMEM)
+HB = pl.BlockSpec(memory_space=pltpu.HBM)
 HIGHEST = lax.Precision.HIGHEST
 BLOCK = (2, N, N)
 STEPS = (1, ENERGIES - 1, ENERGIES // 2)
@@ -74,95 +74,94 @@
     return jnp.broadcast_to(x, (rows, N))
 
 
-def eliminate(rr, ri, first):
-    b, groups = PANEL, PANEL // 8
-    lane = lax.broadcasted_iota(jnp.int32, (b, N), 1)
-    row = lax.broadcasted_iota(jnp.int32, (b, N), 0)
-    for g in range(groups):
-        c0 = first + 8 * g
-        here = (lane >= c0) & (lane < c0 + 8)
-        unit = jnp.where(lane - first == row, 1.0, 0.0)
-        xr = jnp.stack([spread(rr[:, c0 + j : c0 + j + 1], b) for j in range(8)] + [jnp.where(here, unit, rr)])
-        xi = jnp.stack([spread(ri[:, c0 + j : c0 + j + 1], b) for j in range(8)] + [jnp.where(here, 0.0, ri)])
-        for k in range(8):
-            t = 8 * g + k
-            dr, di = xr[0], xi[0]
-            xr, xi = xr[1:], xi[1:]
-            pr, pi = spread(dr[t : t + 1], 8), spread(di[t : t + 1], 8)
-            inv = 1.0 / (pr * pr + pi * pi)
-            qr, qi = (pr * inv)[None], (-pi * inv)[None]
-            shape = (8 - k, 8, N)
-            ar = jnp.broadcast_to(xr[:, t : t + 1, :], shape)
-            ai = jnp.broadcast_to(xi[:, t : t + 1, :], shape)
-            sr, si = qr * ar - qi * ai, qr * ai + qi * ar
-            outr, outi = [], []
-            for v in range(groups):
-                s = slice(8 * v, 8 * v + 8)
-                yr = xr[:, s] - dr[None, s] * sr + di[None, s] * si
-                yi = xi[:, s] - dr[None, s] * si - di[None, s] * sr
-                if v == g:
-                    at_pivot = (row[:8] == k)[None]
-                    yr, yi = jnp.where(at_pivot, sr, yr), jnp.where(at_pivot, si, yi)
-                outr.append(yr)
-                outi.append(yi)
-            xr, xi = jnp.concatenate(outr, 1), jnp.concatenate(outi, 1)
-        rr, ri = xr[0], xi[0]
-    return rr, ri
+def pivot8(x, c0):
+    xr, xi = x
+    lane = lax.broadcasted_iota(jnp.int32, (8, N), 1)
+    row = lax.broadcasted_iota(jnp.int32, (8, N), 0)
+    here = (lane >= c0) & (lane < c0 + 8)
+    unit = jnp.where(lane - c0 == row, 1.0, 0.0)
+    zr = jnp.stack([spread(xr[:, c0 + j : c0 + j + 1], 8) for j in range(8)] + [jnp.where(here, unit, xr)])
+    zi = jnp.stack([spread(xi[:, c0 + j : c0 + j + 1], 8) for j in range(8)] + [jnp.where(here, 0.0, xi)])
+    qr = qi = jnp.zeros((8, N), F32)
+    for k in range(8):
+        dr, di = zr[0], zi[0]
+        zr, zi = zr[1:], zi[1:]
+        pr, pi = spread(dr[k : k + 1], 8), spread(di[k : k + 1], 8)
+        inv = 1.0 / (pr * pr + pi * pi)
+        at_pivot = row == k
+        fr = jnp.where(at_pivot, 0.0, dr * pr + di * pi)[None]
+        fi = jnp.where(at_pivot, 0.0, di * pr - dr * pi)[None]
+        qr = jnp.where(at_pivot, pr * inv, qr)
+        qi = jnp.where(at_pivot, -pi * inv, qi)
+        shape = (8 - k, 8, N)
+        ar = jnp.broadcast_to(zr[:, k : k + 1, :], shape)
+        ai = jnp.broadcast_to(zi[:, k : k + 1, :], shape)
+        zr = zr - (fr * ar - fi * ai) * inv[None]
+        zi = zi - (fr * ai + fi * ar) * inv[None]
+    return qr * zr[0] - qi * zi[0], qr * zi[0] + qi * zr[0]
+
+
+def follow(x, solved, c0):
+    xr, xi = x
+    rows = xr.shape[0]
+    lane = lax.broadcasted_iota(jnp.int32, (rows, N), 1)
+    here = (lane >= c0) & (lane < c0 + 8)
+    yr, yi = jnp.where(here, 0.0, xr), jnp.where(here, 0.0, xi)
+    for k in range(8):
+        cr, ci = spread(xr[:, c0 + k : c0 + k + 1], rows), spread(xi[:, c0 + k : c0 + k + 1], rows)
+        sr, si = spread(solved[0][k : k + 1], rows), spread(solved[1][k : k + 1], rows)
+        yr, yi = yr - (cr * sr - ci * si), yi - (cr * si + ci * sr)
+    return yr, yi
 
 
 def inverse(a):
     ar, ai = a
     b = PANEL
     lane = lax.broadcasted_iota(jnp.int32, (N, N), 1)
-    d = functools.partial(jnp.dot, preferred_element_type=F32)
-    ahead = (ar[:b], ai[:b])
+
+    def groups(first):
+        return [(ar[r : r + 8], ai[r : r + 8]) for r in range(first, first + b, 8)]
+
+    panel = groups(0)
     for f in range(0, N, b):
-        pr, pi = eliminate(*ahead, f)
+        n0 = f + b
+        others = groups(n0) if n0 < N else []
+        for g in range(b // 8):
+            c0 = f + 8 * g
+            solved = pivot8(panel[g], c0)
+            panel = [solved if v == g else follow(x, solved, c0) for v, x in enumerate(panel)]
+            others = [follow(x, solved, c0) for x in others]
+        pr = jnp.concatenate([x[0] for x in panel], 0)
+        pi = jnp.concatenate([x[1] for x in panel], 0)
         inside = (lane >= f) & (lane < f + b)
         zr, zi = jnp.where(inside, 0.0, ar), jnp.where(inside, 0.0, ai)
-        ahead = None
-        n0 = f + b
-        if n0 < N:
-            yr, yi = zr[n0 : n0 + b], zi[n0 : n0 + b]
-            for k in range(b):
-                cr = spread(ar[n0 : n0 + b, f + k : f + k + 1], b)
-                ci = spread(ai[n0 : n0 + b, f + k : f + k + 1], b)
-                sr, si = spread(pr[k : k + 1], b), spread(pi[k : k + 1], b)
-                yr, yi = yr - cr * sr + ci * si, yi - cr * si - ci * sr
-            ahead = (yr, yi)
-        lh, ll = split(jnp.concatenate([ar, ai], 1))
-        prh, prl = split(pr)
-        pih, pil = split(pi)
 
         def gap(rows):
-            return [jnp.zeros((rows, 2 * N), jnp.bfloat16)] if rows else []
-
-        def right(xr, xi):
-            return jnp.concatenate(
-                gap(f)
-                + [jnp.concatenate([xr, xi], 1)]
-                + gap(N - b)
-                + [jnp.concatenate([-xi, xr], 1)]
-                + gap(N - b - f),
-                0,
-            )
-
-        rh, rl = right(prh, pih), right(prl, pil)
-        change = d(lh, rh) + (d(ll, rh) + d(lh, rl))
-
-        def rows(z, ch, panel, following):
+            return [jnp.zeros((rows, 2 * N), F32)] if rows else []
+
+        right = jnp.concatenate(
+            gap(f)
+            + [jnp.concatenate([pr, pi], 1)]
+            + gap(N - b)
+            + [jnp.concatenate([-pi, pr], 1)]
+            + gap(N - b - f),
+            0,
+        )
+        change = dot6(jnp.concatenate([ar, ai], 1), right)
+
+        def rows(z, ch, part):
             new = z - ch
-            blocks = [new[:f], panel] + ([new[n0:]] if following is None else [following, new[n0 + b :]])
+            blocks = [new[:f]] + [x[part] for x in panel + others] + [new[f + 8 * len(panel + others) :]]
             return jnp.concatenate([x for x in blocks if x.shape[0]], 0)
 
-        ar = rows(zr, change[:, :N], pr, None if ahead is None else ahead[0])
-        ai = rows(zi, change[:, N:], pi, None if ahead is None else ahead[1])
+        ar, ai = rows(zr, change[:, :N], 0), rows(zi, change[:, N:], 1)
+        panel = others
     return ar, ai
 
 
 def kernel(
-    ham, coupling, contact, pattern, mode_weight, mode_offset, out,
-    ham_in, link_in, last_in, s_ref, a_ref, b_ref, h_ref, g_ref, p_ref, q_ref, e_ref, f_ref, u_ref,
+    ham_hbm, coupling_hbm, contact_hbm, pattern_hbm, weight_hbm, offset_hbm, out,
+    ham, coupling, contact, pattern, mode_weight, mode_offset, local, ham_in, link_in, last_in, s_ref, a_ref, b_ref, h_ref, g_ref, p_ref, q_ref, e_ref, f_ref, u_ref,
     part, schur, schur_in, join, x_ref, gee, diag, got, send, recv, esend, erecv,
 ):
     space, me = lax.axis_index("space"), lax.axis_index("energy")
@@ -184,21 +183,43 @@
             src, dst, send.at[i], recv.at[i], device_id=to, device_id_type=MESH
         )
 
+    loads = [
+        pltpu.make_async_copy(src, dst, local.at[i])
+        for i, (src, dst) in enumerate(
+            [
+                (ham_hbm, ham),
+                (coupling_hbm, coupling),
+                (contact_hbm, contact),
+                (pattern_hbm, pattern),
+                (weight_hbm, mode_weight),
+                (offset_hbm, mode_offset),
+            ]
+        )
+    ]
+    for load in loads:
+        load.start()
     barrier = pltpu.get_barrier_semaphore()
     for partner in [other] + ahead + behind + targets:
         pl.semaphore_signal(barrier, inc=1, device_id=partner, device_id_type=MESH)
     pl.semaphore_wait(barrier, 8)
 
-    send_ham = remote(ham, ham_in, 0, other)
-    send_link = remote(coupling, link_in, 1, other)
-    last = [remote(coupling.at[1], last_in, 2 + i, ahead[i]) for i in range(2)]
-    send_ham.start()
-    send_link.start()
+    near = jnp.where(right, 1, 0)
+    far = 1 - near
+    first_block = remote(ham_hbm.at[near], ham_in.at[near], 0, other)
+    first_link = remote(coupling_hbm.at[1], link_in.at[1], 1, other)
+    last = [remote(coupling_hbm.at[1], last_in, 2 + i, ahead[i]) for i in range(2)]
+    next_link = remote(coupling_hbm.at[0], link_in.at[0], 7, other)
+    next_block = remote(ham_hbm.at[far], ham_in.at[far], 8, other)
+    first_block.start()
+    first_link.start()
 
     @pl.when(core == 1)
     def _():
         last[0].start()
         last[1].start()
+
+    next_link.start()
+    next_block.start()
 
     energy = -2.0 + 4.0 * (me.astype(F32) + 0.5) / ENERGIES
     eye = jnp.where(
@@ -220,35 +241,41 @@
     def link_slot(b):
         return jnp.where(right, jnp.where(b == 3, 4, 2 - b), b)
 
+    for load in loads[:3]:
+        load.wait()
     for i in range(2):
         place_block(ham, i, core * 2 + i)
         place_link(get(coupling, i), link_slot(core * 2 + i))
-    send_ham.wait()
-    for i in range(2):
-        place_block(ham_in, i, (1 - core) * 2 + i)
-    send_link.wait()
-    for i in range(2):
-        place_link(get(link_in, i), link_slot((1 - core) * 2 + i))
-
-    @pl.when(core == 1)
-    def _():
-        last[0].wait_send()
-        last[1].wait_send()
-        last[1].wait_recv()
-
-    @pl.when(core == 0)
-    def _():
-        last[0].wait_recv()
-
-    place_link(get(last_in), jnp.where(right, 3, 4))
-    lead, lead_adj = get(b_ref, 4), get(h_ref, 4)
-    own = get(contact)
-    gamma = mul(pick(right, lead, own), pick(right, lead_adj, adj(own)))
+    first_block.wait()
+    place_block(ham_in, near, (1 - core) * 2 + near)
+    first_link.wait()
+    place_link(get(link_in, 1), link_slot((1 - core) * 2 + 1))
+    lead, own = get(b_ref, 4), get(contact)
+    lead = pick(right, lead, own)
+    gamma = mul(lead, adj(lead))
     weight = jnp.where(outer, 0.5, 0.0)
     put(s_ref, (a_ref[0, 0] - weight * gamma[1], a_ref[0, 1] + weight * gamma[0]))
-    put(e_ref, pick(outer, (zero, zero), lead), 0)
-    put(f_ref, pick(outer, (zero, zero), lead_adj), 0)
     put(u_ref, (zero, zero))
+
+    def rest():
+        next_link.wait()
+        place_link(get(link_in, 0), link_slot((1 - core) * 2))
+        next_block.wait()
+        place_block(ham_in, far, (1 - core) * 2 + far)
+
+        @pl.when(core == 1)
+        def _():
+            last[0].wait_send()
+            last[1].wait_send()
+            last[1].wait_recv()
+
+        @pl.when(core == 0)
+        def _():
+            last[0].wait_recv()
+
+        place_link(get(last_in), jnp.where(right, 3, 4))
+        put(e_ref, pick(outer, (zero, zero), get(b_ref, 4)), 0)
+        put(f_ref, pick(outer, (zero, zero), get(h_ref, 4)), 0)
 
     send_schur = remote(schur.at[0], schur_in.at[0], 4, pair)
     send_middle = remote(schur.at[1], schur_in.at[1], 5, middle)
@@ -256,6 +283,10 @@
 
     def level(k, _):
         g = inverse(get(s_ref))
+
+        @pl.when(k == 0)
+        def _():
+            rest()
 
         @pl.when(k < 3)
         def _():
@@ -364,6 +395,8 @@
     def _():
         send_green.wait_send()
 
+    for load in loads[3:]:
+        load.wait()
     half = ENERGIES // 2
     shifts = [
         (jnp.where(me >= 1, 1, 99)),
@@ -393,17 +426,24 @@
     return pl.pallas_call(
         kernel,
         out_shape=jax.ShapeDtypeStruct((1, 2) + BLOCK, F32),
-        in_specs=[VM, VM, VM, VM, SM, SM],
+        in_specs=[HB] * 6,
         out_specs=VM,
-        scratch_shapes=[pltpu.VMEM(b + BLOCK, F32) for b in blocks]
+        scratch_shapes=[pltpu.VMEM(b + BLOCK, F32) for b in ((2,), (2,), ())]
         + [
-            pltpu.SemaphoreType.DMA((7,)),
-            pltpu.SemaphoreType.DMA((7,)),
+            pltpu.VMEM((N, N), jnp.int32),
+            pltpu.SMEM((4,), F32),
+            pltpu.SMEM((4,), jnp.int32),
+            pltpu.SemaphoreType.DMA((6,)),
+        ]
+        + [pltpu.VMEM(b + BLOCK, F32) for b in blocks]
+        + [
+            pltpu.SemaphoreType.DMA((9,)),
+            pltpu.SemaphoreType.DMA((9,)),
             pltpu.SemaphoreType.DMA((3, 2)),
             pltpu.SemaphoreType.DMA((3, 2)),
         ],
         compiler_params=pltpu.CompilerParams(
-            collective_id=0, has_side_effects=True, vmem_limit_bytes=48 << 20
+            collective_id=0, has_side_effects=True, vmem_limit_bytes=56 << 20
         ),
     )(ham_diag, coupling, contact_left, pattern, mode_weight, mode_offset)
 

time: 76.3 us -> 70 us (0.917)
  local copies, waits for them, and re-layouts: 5.66 us -> 1.67 us
  Pallas kernels: 70.1 us -> 67.8 us
    unnamed x13 -> x1, local copies, waits for them, and re-layouts: 5.66 us -> 1.67 us
    pallas_call x1, Pallas kernels: 70.1 us -> 67.8 us  [on_device(): pl.pallas_call(kernel, out_shape=jax.ShapeDtypeStruct((1, 2) + BLOCK, F32...]
where the time goes in v3:
time: 70 us; the launch traced here: 69.5 us
  Pallas kernels  67.8 us (97%)
  local copies, waits for them, and re-layouts  1.67 us (2%)
    pallas_call x1, Pallas kernels, on_device(): pl.pallas_call(kernel, out_shape=jax.ShapeDtypeStruct((1, 2) + BLOCK, F32...  67.8 us
    unnamed x1, local copies, waits for them, and re-layouts  1.67 us

profile of v3, /device:TPU:0, one launch (start us, length us, event | category | flops | bytes accessed | tf_op | source)
XLA Modules:
  0.0 69.5 jit_solution(11092624176348789739)
XLA Ops:
  0.0 67.8 %shard_map.64 = f32[1,2,2,128,128]{4,3,2,1,0:T(8,128)} custom-call(f32[2,2,128,128]{3,2,1,0:T(8,128)} %ham_hbm.1, f32[2,2,128,128]{3,2,1,0:T(8,128)} %coupling_hbm.1, f32[2,128,128]{2,1,0:T(8,128)} %contact_hbm.1, s32[128,128]{1,0:T(8,128)} %pattern_hbm.1, f32[4]{0:T(128)} %weight_hbm.1, s32[4]{0:T(128)} %offset_hbm.1), custom_call_target="tpu_custom_call" | custom-call | tf_op jit(solution)/shard_map/pallas_call | solution.py:426
  67.8 1.7 %copy.8 = f32[1,2,2,128,128]{4,3,2,1,0:T(8,128)} copy(f32[1,2,2,128,128]{4,3,2,1,0:T(8,128)} %shard_map.64) | data formatting | bytes 524288

commit v4 on v3

--- a/solution.py
+++ b/solution.py
@@ -161,7 +161,7 @@
 
 def kernel(
     ham_hbm, coupling_hbm, contact_hbm, pattern_hbm, weight_hbm, offset_hbm, out,
-    ham, coupling, contact, pattern, mode_weight, mode_offset, local, ham_in, link_in, last_in, s_ref, a_ref, b_ref, h_ref, g_ref, p_ref, q_ref, e_ref, f_ref, u_ref,
+    ham, coupling, contact, pattern, mode_weight, mode_offset, local, ham_in, link_in, last_in, s_ref, a_ref, b_ref, h_ref, g_ref, p_ref, q_ref, e_ref, f_ref,
     part, schur, schur_in, join, x_ref, gee, diag, got, send, recv, esend, erecv,
 ):
     space, me = lax.axis_index("space"), lax.axis_index("energy")
@@ -255,7 +255,6 @@
     gamma = mul(lead, adj(lead))
     weight = jnp.where(outer, 0.5, 0.0)
     put(s_ref, (a_ref[0, 0] - weight * gamma[1], a_ref[0, 1] + weight * gamma[0]))
-    put(u_ref, (zero, zero))
 
     def rest():
         next_link.wait()
@@ -300,15 +299,34 @@
                 put(schur, new, 0)
                 send_schur.start()
 
-            q = mul(get(h_ref, k), g, dot3)
             put(p_ref, p, k)
-            put(q_ref, q, k)
-            e, f = get(e_ref, k), get(f_ref, k)
-            put(e_ref, mul(e, p, dot3), k + 1)
-            put(f_ref, mul(q, f, dot3), k + 1)
-            put(u_ref, add(get(u_ref), mul(mul(e, g, dot3), f, dot3)))
-
-        @pl.when((k == 2) & inner_core)
+
+        @pl.when(k == 2)
+        def _():
+            u = (zero, zero)
+            for j in range(3):
+                gj = get(g_ref, j)
+                q = mul(get(h_ref, j), gj, dot3)
+                put(q_ref, q, j)
+                e, f = get(e_ref, j), get(f_ref, j)
+                put(e_ref, mul(e, get(p_ref, j), dot3), j + 1)
+                put(f_ref, mul(q, f, dot3), j + 1)
+                u = add(u, mul(mul(e, gj, dot3), f, dot3))
+            send_schur.wait()
+            put(s_ref, sub(get(schur_in, 0), u))
+
+        @pl.when(k == 3)
+        def _():
+            e3, f3 = get(e_ref, 3), get(f_ref, 3)
+            ke = mul(g, e3)
+            put(schur, sub(get(schur, 0), mul(f3, ke)), 1)
+            send_middle.start()
+            fk = mul(f3, g, dot3)
+            put(join, g, 0)
+            put(join, ke, 1)
+            put(join, fk, 2)
+
+        @pl.when((k == 3) & inner_core)
         def _():
             g2 = get(g_ref, 2)
             put(part, g2, 0, 0)
@@ -322,7 +340,7 @@
             put(part, (zero, zero), 1, 3)
             put(part, (zero, zero), 1, 4)
 
-        @pl.when((k == 2) & jnp.logical_not(inner_core))
+        @pl.when((k == 3) & jnp.logical_not(inner_core))
         def _():
             p0, p1, q0, q1 = get(p_ref, 0), get(p_ref, 1), get(q_ref, 0), get(q_ref, 1)
             w1 = add(get(g_ref, 1), mul(mul(p1, get(g_ref, 2), dot3), q1, dot3))
@@ -339,26 +357,8 @@
             put(part, mul(w0, get(f_ref, 0), dot3), 1, 3)
             put(part, mul(get(e_ref, 0), w0, dot3), 1, 4)
 
-        @pl.when(k == 2)
-        def _():
-            send_schur.wait()
-            put(s_ref, sub(get(schur_in, 0), get(u_ref)))
-
         @pl.when(k == 3)
         def _():
-            e3, f3 = get(e_ref, 3), get(f_ref, 3)
-            ke = mul(g, e3)
-            put(schur, sub(get(schur, 0), mul(f3, ke)), 1)
-            send_middle.start()
-            fk = mul(f3, g, dot3)
-            put(join, g, 0)
-            put(join, ke, 1)
-            put(join, fk, 2)
-            for t in range(2):
-                le, re = get(part, t, 3), get(part, t, 4)
-                put(part, add(get(part, t, 0), mul(mul(le, g, dot3), re, dot3)), t, 0)
-                put(part, add(get(part, t, 1), mul(le, ke, dot3)), t, 1)
-                put(part, add(get(part, t, 2), mul(fk, re, dot3)), t, 2)
             send_middle.wait()
             s_ref[...] = schur_in[1]
 
@@ -371,6 +371,12 @@
             put(gee, add(get(join, 0), mul(get(join, 1), mul(g, get(join, 2)))))
             send_green.start()
             put(x_ref, g)
+            kk, ke, fk = get(join, 0), get(join, 1), get(join, 2)
+            for t in range(2):
+                le, re = get(part, t, 3), get(part, t, 4)
+                put(part, add(get(part, t, 0), mul(mul(le, kk, dot3), re, dot3)), t, 0)
+                put(part, add(get(part, t, 1), mul(le, ke, dot3)), t, 1)
+                put(part, add(get(part, t, 2), mul(fk, re, dot3)), t, 2)
 
         return 0
 
@@ -421,7 +427,7 @@
 
 
 def on_device(ham_diag, coupling, contact_left, mode_weight, mode_offset, pattern):
-    blocks = [(2,), (2,), (), (), (4,), (5,), (5,), (3,), (3,), (3,), (4,), (4,), ()]
+    blocks = [(2,), (2,), (), (), (4,), (5,), (5,), (3,), (3,), (3,), (4,), (4,)]
     blocks += [(2, 5), (2,), (2,), (3,), (), (), (2,), (3, 2)]
     return pl.pallas_call(
         kernel,

time: 70 us -> 69 us (0.986)
  Pallas kernels: 67.8 us -> 66.8 us
    pallas_call x1, Pallas kernels: 67.8 us -> 66.8 us  [on_device(): pl.pallas_call(kernel, out_shape=jax.ShapeDtypeStruct((1, 2) + BLOCK, F32...]
where the time goes in v4:
time: 69 us; the launch traced here: 68.5 us
  Pallas kernels  66.8 us (97%)
  local copies, waits for them, and re-layouts  1.67 us (2%)
    pallas_call x1, Pallas kernels, on_device(): pl.pallas_call(kernel, out_shape=jax.ShapeDtypeStruct((1, 2) + BLOCK, F32...  66.8 us
    unnamed x1, local copies, waits for them, and re-layouts  1.67 us

profile of v4, /device:TPU:0, one launch (start us, length us, event | category | flops | bytes accessed | tf_op | source)
XLA Modules:
  0.0 68.5 jit_solution(13453894803403203613)
XLA Ops:
  0.0 66.8 %shard_map.64 = f32[1,2,2,128,128]{4,3,2,1,0:T(8,128)} custom-call(f32[2,2,128,128]{3,2,1,0:T(8,128)} %ham_hbm.1, f32[2,2,128,128]{3,2,1,0:T(8,128)} %coupling_hbm.1, f32[2,128,128]{2,1,0:T(8,128)} %contact_hbm.1, s32[128,128]{1,0:T(8,128)} %pattern_hbm.1, f32[4]{0:T(128)} %weight_hbm.1, s32[4]{0:T(128)} %offset_hbm.1), custom_call_target="tpu_custom_call" | custom-call | tf_op jit(solution)/shard_map/pallas_call | solution.py:432
  66.8 1.7 %copy.8 = f32[1,2,2,128,128]{4,3,2,1,0:T(8,128)} copy(f32[1,2,2,128,128]{4,3,2,1,0:T(8,128)} %shard_map.64) | data formatting | bytes 524288

commit v5 on v4

--- a/solution.py
+++ b/solution.py
@@ -368,7 +368,7 @@
 
         @pl.when((k == 5) & inner)
         def _():
-            put(gee, add(get(join, 0), mul(get(join, 1), mul(g, get(join, 2)))))
+            put(gee, add(get(join, 0), mul(get(join, 1), mul(g, get(join, 2), dot3), dot3)))
             send_green.start()
             put(x_ref, g)
             kk, ke, fk = get(join, 0), get(join, 1), get(join, 2)
@@ -389,7 +389,7 @@
     x = get(x_ref)
     copies = []
     for t in range(2):
-        put(diag, add(get(part, t, 0), mul(mul(get(part, t, 1), x), get(part, t, 2))), t)
+        put(diag, add(get(part, t, 0), mul(mul(get(part, t, 1), x, dot3), get(part, t, 2), dot3)), t)
         for i, to in enumerate(targets):
             copy = pltpu.make_async_remote_copy(
                 diag.at[t], got.at[i, t], esend.at[i, t], erecv.at[i, t], device_id=to, device_id_type=MESH

time: 69 us -> 68.6 us (level)
  no operation moved by 1% of the time
where the time goes in v5:
time: 68.6 us; the launch traced here: 68.1 us
  Pallas kernels  66.4 us (97%)
  local copies, waits for them, and re-layouts  1.67 us (2%)
    pallas_call x1, Pallas kernels, on_device(): pl.pallas_call(kernel, out_shape=jax.ShapeDtypeStruct((1, 2) + BLOCK, F32...  66.4 us
    unnamed x1, local copies, waits for them, and re-layouts  1.67 us

profile of v5, /device:TPU:0, one launch (start us, length us, event | category | flops | bytes accessed | tf_op | source)
XLA Modules:
  0.0 68.1 jit_solution(7723025893842313161)
XLA Ops:
  0.0 66.4 %shard_map.64 = f32[1,2,2,128,128]{4,3,2,1,0:T(8,128)} custom-call(f32[2,2,128,128]{3,2,1,0:T(8,128)} %ham_hbm.1, f32[2,2,128,128]{3,2,1,0:T(8,128)} %coupling_hbm.1, f32[2,128,128]{2,1,0:T(8,128)} %contact_hbm.1, s32[128,128]{1,0:T(8,128)} %pattern_hbm.1, f32[4]{0:T(128)} %weight_hbm.1, s32[4]{0:T(128)} %offset_hbm.1), custom_call_target="tpu_custom_call" | custom-call | tf_op jit(solution)/shard_map/pallas_call | solution.py:432
  66.4 1.7 %copy.8 = f32[1,2,2,128,128]{4,3,2,1,0:T(8,128)} copy(f32[1,2,2,128,128]{4,3,2,1,0:T(8,128)} %shard_map.64) | data formatting | bytes 524288
